TPU v7x, 32 devices: a whole 2x2x4 slice. The times are simulated.
32 devices in a mesh: section: 2 (over core), dp: 16 (over z, y, x).
Axes of the slice: x: 2, y: 2, z: 4, core: 2. Of those that a mesh axis runs over, the one named last changes fastest.
Arguments:
- inputs: bfloat16 [2, 48, 128, 2000], P(None, 'dp'), may hold values from -9 to 9
- lengths: int32 [2, 16], replicated, may hold values from 32 to 128, as said below
- weights: float32 [2, 4000000], P('section', 'dp'), may hold values from -0.125 to 0.125
- scales: float32 [2, 2000], P('section'), may hold values from 0.5 to 1.5
- biases: float32 [2, 2000], P('section'), may hold values from -2 to 2
- decays: float32 [2, 2000], P('section'), may hold values from 0.1 to 0.8
- cotangent: bfloat16 [2, 48, 128, 2000], P(None, 'dp'), may hold values from -9 to 9
Outputs:
- activations: bfloat16 [2, 2, 48, 128, 2000], P('section', None, 'dp')
- input_grads: bfloat16 [2, 2, 48, 128, 2000], P('section', None, 'dp')
- weight_grads: float32 [2, 4000000], P('section', 'dp')
- scale_grads: float32 [2, 2000], P('section')
- bias_grads: float32 [2, 2000], P('section')
- decay_grads: float32 [2, 2000], P('section')
Inputs may be any that keep to these rules, and one draw needn't show every extreme that they name: `lengths`: all 3 views of a group share one length; in every micro-batch some group has exactly 128 valid frames.
All inputs are finite; a program needn't handle non-finite values.
Results may differ from a plain program's by a relative error of at most 0.0062.
Values may be sent and summed in bfloat16 or wider, within the bound.
No kernel may reach another device: no remote copies, remote signals or barrier semaphores. Data moves between devices by JAX's collectives and lax.ppermute only.
A program may use at most 256 MiB of HBM per device.

v0:
```python
from functools import partial

import jax
import jax.numpy as jnp
from jax import lax
from jax.sharding import PartitionSpec as P

EPSILON = 1e-05


def from_behind(shard, axis, by):
    count = lax.axis_size(axis)
    pairs = [(i, i + by) for i in range(count) if 0 <= i + by < count]
    return lax.ppermute(shard, axis, pairs)


def advance_state(decay_rate, state, value):
    fresh = jax.nn.silu(value + decay_rate * state)
    return (fresh, fresh)


def retreat_state(decay_rate, carry, item):
    local_value, slope_value = item
    fresh = slope_value * (local_value + decay_rate * carry)
    return (fresh, fresh)


def place_slot(store, value, slot_index, active_flag):
    updated = lax.dynamic_update_index_in_dim(store, value, slot_index, 0)
    return jnp.where(active_flag, updated, store)


def per_device(inputs, lengths, weights, scales, biases, decays, cotangent):
    section_index = lax.axis_index("section")
    dp_index = lax.axis_index("dp")
    micro_count, view_count, frame_count, feature_width = inputs.shape
    row_total = view_count * frame_count
    weight_full = lax.all_gather(weights.astype(jnp.bfloat16), "dp", axis=1, tiled=True).reshape(
        feature_width, feature_width
    )
    gain_vector = scales[0]
    shift_bias = biases[0]
    decay_rate = decays[0]
    own_lengths = lax.dynamic_index_in_dim(lengths, dp_index, 1, keepdims=False)
    frame_masks = (jnp.arange(frame_count)[None, :] < own_lengths[:, None]).astype(jnp.float32)
    frame_totals = view_count * jnp.sum(lengths, axis=1).astype(jnp.float32)

    def rows_of(frame_mask):
        return jnp.broadcast_to(frame_mask[None, :], (view_count, frame_count)).reshape(
            row_total, 1
        )

    def forward_layer(layer_input, frame_mask, frame_total):
        flat_input = layer_input.reshape(row_total, feature_width)
        projected = jnp.dot(flat_input, weight_full, preferred_element_type=jnp.float32)
        row_mask = rows_of(frame_mask)
        first_sum, second_sum = lax.psum(
            (
                jnp.sum(row_mask * projected, axis=0),
                jnp.sum(row_mask * projected * projected, axis=0),
            ),
            "dp",
        )
        centre = first_sum / frame_total
        variance = second_sum / frame_total - centre * centre
        inverse_std = lax.rsqrt(variance + EPSILON)
        normed = (projected - centre) * inverse_std
        drive_term = (
            (gain_vector * normed + shift_bias)
            .reshape(view_count, frame_count, feature_width)
            .transpose(1, 0, 2)
        )
        _, states = lax.scan(
            partial(advance_state, decay_rate),
            jnp.zeros((view_count, feature_width), jnp.float32),
            drive_term,
            unroll=8,
        )
        hidden = states.transpose(1, 0, 2)
        output = layer_input.astype(jnp.float32) + frame_mask[None, :, None] * hidden
        return (output, normed, hidden, inverse_std)

    def backward_layer(upstream, layer_input, normed, hidden, inverse_std, frame_mask, frame_total):
        row_mask = rows_of(frame_mask)
        drive_term = (gain_vector * normed + shift_bias).reshape(
            view_count, frame_count, feature_width
        )
        previous = jnp.concatenate(
            [jnp.zeros((view_count, 1, feature_width), jnp.float32), hidden[:, :-1]], axis=1
        )
        before = drive_term + decay_rate * previous
        logistic = jax.nn.sigmoid(before)
        slope_value = logistic * (1.0 + before * (1.0 - logistic))
        local_grad = frame_mask[None, :, None] * upstream
        _, pre_grads = lax.scan(
            partial(retreat_state, decay_rate),
            jnp.zeros((view_count, feature_width), jnp.float32),
            (local_grad.transpose(1, 0, 2), slope_value.transpose(1, 0, 2)),
            reverse=True,
            unroll=8,
        )
        pre_grad = pre_grads.transpose(1, 0, 2).reshape(row_total, feature_width)
        gain_part = jnp.sum(pre_grad * normed, axis=0)
        bias_part = jnp.sum(pre_grad, axis=0)
        decay_part = jnp.sum(pre_grad * previous.reshape(row_total, feature_width), axis=0)
        normed_grad = gain_vector * pre_grad
        first_back, second_back = lax.psum(
            (
                jnp.sum(row_mask * normed_grad, axis=0),
                jnp.sum(row_mask * normed_grad * normed, axis=0),
            ),
            "dp",
        )
        proj_grad = (
            inverse_std
            * (
                normed_grad
                - row_mask * first_back / frame_total
                - row_mask * normed * second_back / frame_total
            )
        ).astype(jnp.bfloat16)
        flat_input = layer_input.reshape(row_total, feature_width)
        weight_part = lax.dot_general(
            flat_input, proj_grad, (((0,), (0,)), ((), ())), preferred_element_type=jnp.float32
        )
        carried = lax.dot_general(
            proj_grad, weight_full, (((1,), (1,)), ((), ())), preferred_element_type=jnp.float32
        )
        input_grad = upstream + carried.reshape(view_count, frame_count, feature_width)
        return (input_grad, weight_part, gain_part, bias_part, decay_part)

    block_shape = (view_count, frame_count, feature_width)
    incoming = jnp.zeros(block_shape, jnp.bfloat16)
    act_store = jnp.zeros((micro_count,) + block_shape, jnp.bfloat16)
    input_store = jnp.zeros((micro_count,) + block_shape, jnp.bfloat16)
    normed_store = jnp.zeros((micro_count, row_total, feature_width), jnp.float32)
    hidden_store = jnp.zeros((micro_count,) + block_shape, jnp.float32)
    scale_store = jnp.zeros((micro_count, feature_width), jnp.float32)
    for tick_index in range(micro_count + 1):
        position = tick_index - section_index
        active_flag = (position >= 0) & (position < micro_count)
        slot_index = jnp.clip(position, 0, micro_count - 1)
        source = lax.dynamic_index_in_dim(inputs, slot_index, 0, keepdims=False)
        layer_input = jnp.where(section_index == 0, source, incoming)
        output, normed, hidden, inverse_std = forward_layer(
            layer_input, frame_masks[slot_index], frame_totals[slot_index]
        )
        sending = output.astype(jnp.bfloat16)
        act_store = place_slot(act_store, sending, slot_index, active_flag)
        input_store = place_slot(input_store, layer_input, slot_index, active_flag)
        normed_store = place_slot(normed_store, normed, slot_index, active_flag)
        hidden_store = place_slot(hidden_store, hidden, slot_index, active_flag)
        scale_store = place_slot(scale_store, inverse_std, slot_index, active_flag)
        if tick_index < micro_count:
            incoming = from_behind(sending, "section", 1)
    incoming_grad = jnp.zeros(block_shape, jnp.bfloat16)
    grad_store = jnp.zeros((micro_count,) + block_shape, jnp.bfloat16)
    weight_total = jnp.zeros((feature_width, feature_width), jnp.float32)
    gain_total = jnp.zeros((feature_width,), jnp.float32)
    bias_total = jnp.zeros((feature_width,), jnp.float32)
    decay_total = jnp.zeros((feature_width,), jnp.float32)
    for tick_index in range(micro_count + 1):
        position = tick_index - (1 - section_index)
        active_flag = (position >= 0) & (position < micro_count)
        slot_index = jnp.clip(position, 0, micro_count - 1)
        source = lax.dynamic_index_in_dim(cotangent, slot_index, 0, keepdims=False)
        upstream = jnp.where(section_index == 1, source, incoming_grad).astype(jnp.float32)
        input_grad, weight_part, gain_part, bias_part, decay_part = backward_layer(
            upstream,
            input_store[slot_index],
            normed_store[slot_index],
            hidden_store[slot_index],
            scale_store[slot_index],
            frame_masks[slot_index],
            frame_totals[slot_index],
        )
        flag_value = active_flag.astype(jnp.float32)
        gain_total = gain_total + flag_value * gain_part
        bias_total = bias_total + flag_value * bias_part
        decay_total = decay_total + flag_value * decay_part
        weight_total = weight_total + flag_value * weight_part
        sending = input_grad.astype(jnp.bfloat16)
        grad_store = place_slot(grad_store, sending, slot_index, active_flag)
        if tick_index < micro_count:
            incoming_grad = from_behind(sending, "section", -1)
    weight_shard = lax.psum_scatter(
        weight_total.reshape(1, -1), "dp", scatter_dimension=1, tiled=True
    )
    scale_sum, bias_sum, decay_sum = lax.psum((gain_total, bias_total, decay_total), "dp")
    return (
        act_store[None],
        grad_store[None],
        weight_shard,
        scale_sum[None],
        bias_sum[None],
        decay_sum[None],
    )


def solution(mesh):
    placed = (
        P(None, "dp", None, None),
        P(),
        P("section", "dp"),
        P("section", None),
        P("section", None),
        P("section", None),
        P(None, "dp", None, None),
    )
    return jax.shard_map(
        per_device,
        mesh=mesh,
        in_specs=placed,
        out_specs=(
            P("section", None, "dp", None, None),
            P("section", None, "dp", None, None),
            P("section", "dp"),
            P("section", None),
            P("section", None),
            P("section", None),
        ),
        check_vma=False,
    )
```

profile of v0, /device:TPU:19, one launch (start us, length us, event | category | flops | bytes accessed | tf_op | source)
XLA Modules:
  0.0 2021.5 jit_solution(9529747589707520432)
XLA Ops:
  7.2 8.4 convert_reduce_fusion
  21.1 8.8 dynamic-update-slice.20
  42.4 236.8 %all-reduce.14.cloned.1.call-done = bf16[4000000]{0:T(1024)(128)(2,1)} async-done(((bf16[4000000]{0:T(1024)(128)(2,1)}), bf16[4000000]{0:T(1024)(128)(2,1)}) %all-reduce.14.cloned.1.call-update) | async-done | bytes 8000016
  279.1 16.1 reshape.546
  295.2 10.1 fusion.78
  305.4 48.8 %all-reduce.10 = (f32[2000]{0:T(1024)S(1)}, f32[2000]{0:T(1024)S(1)}) all-reduce(f32[2000]{0:T(1024)S(1)} %get-tuple-element.665, f32[2000]{0:T(1024)S(1)} %get-tuple-element.664), channel_id=1, replica_groups=mesh['section'=2,'dp'=16] {'dp'}, use_global_device_ids=true, to_apply=%region_1.2 | all-reduce | flops 4000 | bytes 32000 | tf_op jit(solution)/shard_map/psum | solution.py:57
  363.1 55.8 %while.90 = (s32[]{:T(128)}, f32[3,2000]{1,0:T(4,128)S(1)}, f32[16,8,3,2000]{3,1,0,2:T(8,128)}, f32[16,8,3,2000]{3,1,0,2:T(8,128)}, f32[1,2000]{1,0:T(1,128)S(1)...) while((s32[]{:T(128)}, f32[3,2000]{1,0:T(4,128)S(1)}, ...), condition=%wide.region_6.7_spmd.clone, body=%wide.region_5.6_spmd.clone.sunk | while | flops 486009 | bytes 1803729 | solution.py:73
  434.2 16.0 reshape.579
  466.3 10.1 multiply_reduce_fusion.1
  476.4 59.3 %all-reduce.9 = (f32[2000]{0:T(1024)S(1)}, f32[2000]{0:T(1024)S(1)}) all-reduce(f32[2000]{0:T(1024)S(1)} %get-tuple-element.663, f32[2000]{0:T(1024)S(1)} %get-tuple-element.662), channel_id=1, replica_groups=mesh['section'=2,'dp'=16] {'dp'}, use_global_device_ids=true, to_apply=%region_10.11 | all-reduce | flops 4000 | bytes 32000 | tf_op jit(solution)/shard_map/psum | solution.py:57
  547.2 53.7 %while.91 = (s32[]{:T(128)}, f32[3,2000]{1,0:T(4,128)S(1)}, f32[16,8,3,2000]{3,2,1,0:T(4,128)}, f32[16,8,3,2000]{3,1,0,2:T(8,128)}, f32[1,2000]{1,0:T(1,128)S(1)...) while((s32[]{:T(128)}, f32[3,2000]{1,0:T(4,128)S(1)}, ...), condition=%wide.region_12.13_spmd.clone, body=%wide.region_11.12_spmd.clone.sunk | while | flops 486009 | bytes 1869265 | solution.py:73
  600.9 4.9 copy.98
  605.8 5.1 fusion.110
  612.3 5.0 fusion.82
  621.2 21.8 %collective-permute-done.1 = bf16[3,128,2000]{1,2,0:T(8,128)(2,1)} collective-permute-done((bf16[3,128,2000]{1,2,0:T(8,128)(2,1)}, bf16[3,128,2000]{1,2,0:T(8,128)(2,1)}, u32[]{:S(2)}, u32[]{:S(2)}) %collective-permute-start.1) | collective-permute-done | bytes 1536032 | tf_op jit(solution)/shard_map/ppermute | solution.py:14
  650.0 10.1 multiply_reduce_fusion
  660.2 58.2 %all-reduce.8 = (f32[2000]{0:T(1024)S(1)}, f32[2000]{0:T(1024)S(1)}) all-reduce(f32[2000]{0:T(1024)S(1)} %get-tuple-element.661, f32[2000]{0:T(1024)S(1)} %get-tuple-element.660), channel_id=1, replica_groups=mesh['section'=2,'dp'=16] {'dp'}, use_global_device_ids=true, to_apply=%region_16.17 | all-reduce | flops 4000 | bytes 32000 | tf_op jit(solution)/shard_map/psum | solution.py:57
  728.2 53.5 %while.92 = (s32[]{:T(128)}, f32[3,2000]{1,0:T(4,128)S(1)}, f32[16,8,3,2000]{3,2,1,0:T(4,128)}, f32[16,8,3,2000]{3,1,0,2:T(8,128)}, f32[1,2000]{1,0:T(1,128)S(1)...) while((s32[]{:T(128)}, f32[3,2000]{1,0:T(4,128)S(1)}, ...), condition=%wide.region_18.19_spmd.clone, body=%wide.region_17.18_spmd.clone.sunk | while | flops 486009 | bytes 1869265 | solution.py:73
  781.7 5.1 copy.103
  790.5 7.0 constant_dynamic-slice_fusion.73
  815.9 7.5 dynamic-slice_bitcast_fusion
  830.7 11.7 multiply_bitcast_fusion
  849.0 61.4 %while.93 = (s32[]{:T(128)}, f32[3,2000]{1,0:T(4,128)S(1)}, f32[16,8,3,2000]{3,2,1,0:T(4,128)}, f32[16,8,3,2000]{3,1,0,2:T(8,128)}, f32[16,8,3,2000]{3,1,0,2:T(8...) while((s32[]{:T(128)}, f32[3,2000]{1,0:T(4,128)S(1)}, ...), condition=%wide.region_20.21_spmd.clone, body=%wide.region_19.20_spmd.clone.sunk | while | flops 228010 | bytes 2538412 | solution.py:95
  910.3 5.2 copy.112
  915.6 5.7 copy.153
  924.9 6.3 fusion.91
  935.5 57.8 %all-reduce.7 = (f32[2000]{0:T(1024)S(1)}, f32[2000]{0:T(1024)S(1)}) all-reduce(f32[2000]{0:T(1024)S(1)} %fusion.90, f32[2000]{0:T(1024)S(1)} %get-tuple-element.668), channel_id=1, replica_groups=mesh['section'=2,'dp'=16] {'dp'}, use_global_device_ids=true, to_apply=%region_24.25 | all-reduce | flops 4000 | bytes 32000 | tf_op jit(solution)/shard_map/psum | solution.py:107
  1001.7 9.6 bitcast_dynamic-update-slice_fusion.55
  1011.3 36.2 %collective-permute-start.2 = (bf16[3,128,2000]{1,2,0:T(8,128)(2,1)}, bf16[3,128,2000]{1,2,0:T(8,128)(2,1)}, u32[]{:S(2)}, u32[]{:S(2)}) collective-permute-start(bf16[3,128,2000]{1,2,0:T(8,128)(2,1)} %get-tuple-element.940), channel_id=1, source_target_pairs={{16,0},{17,1},{18,2},{19,3},{20,4},{21,5},{22,6},{23,7},{24,8},{25... | collective-permute-start | bytes 4608008 | tf_op jit(solution)/shard_map/ppermute | solution.py:14
  1062.4 67.5 %while.94 = (s32[]{:T(128)}, f32[3,2000]{1,0:T(4,128)S(1)}, f32[16,8,3,2000]{3,2,1,0:T(4,128)}, f32[16,8,3,2000]{3,1,0,2:T(8,128)}, f32[16,8,3,2000]{3,1,0,2:T(8...) while((s32[]{:T(128)}, f32[3,2000]{1,0:T(4,128)S(1)}, ...), condition=%wide.region_26.27_spmd.clone, body=%wide.region_25.26_spmd.clone.sunk | while | flops 228010 | bytes 2538412 | solution.py:95
  1134.8 5.7 copy.156
  1144.1 6.4 fusion.88
  1151.5 58.1 %all-reduce.6 = (f32[2000]{0:T(1024)S(1)}, f32[2000]{0:T(1024)S(1)}) all-reduce(f32[2000]{0:T(1024)S(1)} %fusion.87, f32[2000]{0:T(1024)S(1)} %get-tuple-element.671), channel_id=1, replica_groups=mesh['section'=2,'dp'=16] {'dp'}, use_global_device_ids=true, to_apply=%region_30.31 | all-reduce | flops 4000 | bytes 32000 | tf_op jit(solution)/shard_map/psum | solution.py:107
  1209.6 5.1 multiply_convert_fusion.1
  1214.8 10.7 fusion.109
  1225.5 15.7 collective-permute-start.3
  1260.6 11.9 fusion.135
  1278.6 12.1 fusion.136
  1299.8 63.7 %while.95 = (s32[]{:T(128)}, f32[3,2000]{1,0:T(4,128)S(1)}, f32[16,8,3,2000]{3,2,1,0:T(4,128)}, f32[16,8,3,2000]{3,1,0,2:T(8,128)}, f32[16,8,3,2000]{3,1,0,2:T(8...) while((s32[]{:T(128)}, f32[3,2000]{1,0:T(4,128)S(1)}, ...), condition=%wide.region_32.33_spmd.clone, body=%wide.region_31.32_spmd.clone.sunk | while | flops 228010 | bytes 2538412 | solution.py:95
  1368.3 5.7 copy.159
  1377.5 4.9 fusion.85
  1389.0 59.1 %all-reduce.5 = (f32[2000]{0:T(1024)S(1)}, f32[2000]{0:T(1024)S(1)}, f32[1,2000]{1,0:T(1,128)}, f32[1,2000]{1,0:T(1,128)}, f32[1,2000]{1,0:T(1,128)}) all-reduce(f32[2000]{0:T(1024)S(1)} %fusion.84, f32[2000]{0:T(1024)S(1)} %get-tuple-element.674, f32[1,2000]{1,0:T(1,128)S(1)} %bitcast.1322, ...), channel_id=1, replica_groups=mesh['section'=2,'dp'=16] {'dp'}, use_global_device_ids=true, to_apply=%region_36.37 | all-reduce | flops 10000 | bytes 80000 | tf_op jit(solution)/shard_map/psum | solution.py:107
  1448.2 5.2 multiply_convert_fusion
  1455.3 18.0 multiply_add_fusion
  1473.3 19.5 reshape.586
  1492.8 60.9 %reshape.570 = f32[1,4000000]{1,0:T(1,128)} reshape(f32[4000000]{0:T(1024)} %reshape.586) | data formatting | bytes 32000000 | tf_op jit(solution)/shard_map/reshape | solution.py:187
  1564.9 6.3 fusion.102
  1571.2 439.2 %all-reduce.16.cloned.1.call-done = f32[1,4000000]{1,0:T(1,128)} async-done(((f32[1,4000000]{1,0:T(1,128)}), f32[1,4000000]{1,0:T(1,128)}) %all-reduce.16.cloned.1.call-update) | async-done | bytes 16000016
  (1217 shorter events, 586.6 us)
Async XLA Ops:
  7.2 272.0 %all-reduce.14.cloned.1.call-start = ((), (), s32[]{:S(2)}) async-start(), calls=%async_computation | async-start | bytes 16003072
  29.9 1980.5 %all-reduce.16.cloned.1.call-start = ((), (), s32[]{:S(2)}) async-start(), calls=%async_computation.1 | async-start | bytes 32000000
  38.4 395.8 %copy-start.44 = (f32[128]{0:T(128)}, f32[128]{0:T(128)S(1)}, u32[]{:S(2)}) copy-start(f32[128]{0:T(128)S(1)} %get-tuple-element.925) | copy-start | bytes 1540
  38.4 886.6 %copy-start.34 = (f32[128]{0:T(128)}, f32[128]{0:T(128)S(1)}, u32[]{:S(2)}) copy-start(f32[128]{0:T(128)S(1)} %get-tuple-element.924) | copy-start | bytes 1540
  295.2 60.1 %copy-start.26 = (f32[1,2000]{1,0:T(1,128)S(1)}, f32[1,2000]{1,0:T(1,128)}, u32[]{:S(2)}) copy-start(f32[1,2000]{1,0:T(1,128)} %param.22) | copy-start | bytes 24004
  295.2 60.1 %copy-start.27 = (f32[1,2000]{1,0:T(1,128)S(1)}, f32[1,2000]{1,0:T(1,128)}, u32[]{:S(2)}) copy-start(f32[1,2000]{1,0:T(1,128)} %param.23) | copy-start | bytes 24004
  359.5 3.6 copy-start
  422.5 3.0 copy-start.6
  429.1 30.7 %collective-permute-start = (bf16[3,128,2000]{1,2,0:T(8,128)(2,1)}, bf16[3,128,2000]{1,2,0:T(8,128)(2,1)}, u32[]{:S(2)}, u32[]{:S(2)}) collective-permute-start(bf16[3,128,2000]{1,2,0:T(8,128)(2,1)} %get-tuple-element.806), channel_id=1, source_target_pairs={{0,16},{1,17},{2,18},{3,19},{4,20},{5,21},{6,22},{7,23},{8,24},{9,... | collective-permute-start | bytes 4608008 | tf_op jit(solution)/shard_map/ppermute | solution.py:14
  452.5 5.0 copy-start.1
  452.5 5.0 copy-start.10
  610.9 32.1 %collective-permute-start.1 = (bf16[3,128,2000]{1,2,0:T(8,128)(2,1)}, bf16[3,128,2000]{1,2,0:T(8,128)(2,1)}, u32[]{:S(2)}, u32[]{:S(2)}) collective-permute-start(bf16[3,128,2000]{1,2,0:T(8,128)(2,1)} %get-tuple-element.804), channel_id=1, source_target_pairs={{0,16},{1,17},{2,18},{3,19},{4,20},{5,21},{6,22},{7,23},{8,24},{9,... | collective-permute-start | bytes 4608008 | tf_op jit(solution)/shard_map/ppermute | solution.py:14
  612.3 5.0 copy-start.12
  617.3 25.7 %copy-start.15 = (bf16[2,3,128,2000]{2,3,1,0:T(8,128)(2,1)S(1)}, bf16[2,3,128,2000]{2,3,1,0:T(8,128)(2,1)}, u32[]{:S(2)}) copy-start(bf16[2,3,128,2000]{2,3,1,0:T(8,128)(2,1)} %param.19) | copy-start | bytes 9216004
  646.4 13.8 copy-start.2
  781.7 5.1 copy-start.13
  797.5 8.2 copy-start.4
  924.9 7.0 copy-start.41
  932.0 61.3 %copy-start.35 = (f32[128]{0:T(128)S(1)}, f32[128]{0:T(128)}, u32[]{:S(2)}) copy-start(f32[128]{0:T(128)} %copy-done.34) | copy-start | bytes 1540
  998.2 13.1 copy-start.21
  998.2 3.5 copy-start.16
  1001.7 45.8 %copy-start.39 = (f32[128]{0:T(128)S(1)}, f32[128]{0:T(128)}, u32[]{:S(2)}) copy-start(f32[128]{0:T(128)} %get-tuple-element.923) | copy-start | bytes 1540
  1001.7 46.4 %copy-start.36 = (f32[128]{0:T(128)S(1)}, f32[128]{0:T(128)}, u32[]{:S(2)}) copy-start(f32[128]{0:T(128)} %get-tuple-element.922) | copy-start | bytes 1540
  1011.3 41.1 %collective-permute-start.2 = (bf16[3,128,2000]{1,2,0:T(8,128)(2,1)}, bf16[3,128,2000]{1,2,0:T(8,128)(2,1)}, u32[]{:S(2)}, u32[]{:S(2)}) collective-permute-start(bf16[3,128,2000]{1,2,0:T(8,128)(2,1)} %get-tuple-element.940), channel_id=1, source_target_pairs={{16,0},{17,1},{18,2},{19,3},{20,4},{21,5},{22,6},{23,7},{24,8},{25... | collective-permute-start | bytes 4608008 | tf_op jit(solution)/shard_map/ppermute | solution.py:14
  1140.5 3.6 copy-start.40
  1144.1 6.4 copy-start.5
  1144.1 6.4 copy-start.11
  1144.1 6.4 copy-start.43
  1209.6 5.2 copy-start.17
  1214.8 10.8 copy-start.23
  1214.8 26.5 %copy-start.3 = (bf16[2,3,128,2000]{2,3,1,0:T(8,128)(2,1)S(1)}, bf16[2,3,128,2000]{2,3,1,0:T(8,128)(2,1)}, u32[]{:S(2)}) copy-start(bf16[2,3,128,2000]{2,3,1,0:T(8,128)(2,1)} %copy-done.2) | copy-start | bytes 9216004
  1225.5 65.2 %collective-permute-start.3 = (bf16[3,128,2000]{1,2,0:T(8,128)(2,1)}, bf16[3,128,2000]{1,2,0:T(8,128)(2,1)}, u32[]{:S(2)}, u32[]{:S(2)}) collective-permute-start(bf16[3,128,2000]{1,2,0:T(8,128)(2,1)} %get-tuple-element.942), channel_id=1, source_target_pairs={{16,0},{17,1},{18,2},{19,3},{20,4},{21,5},{22,6},{23,7},{24,8},{25... | collective-permute-start | bytes 4608008 | tf_op jit(solution)/shard_map/ppermute | solution.py:14
  1278.6 12.1 copy-start.18
  1278.6 12.1 copy-start.37
  1374.0 3.5 copy-start.38
  1382.5 2.9 copy-start.42
  1385.3 3.6 copy-start.28
  1385.3 3.6 copy-start.30
  1385.3 3.6 copy-start.31
  1385.4 3.6 copy-start.32
  1385.4 3.6 copy-start.33
  1385.4 62.8 %copy-start.29 = (f32[1,2000]{1,0:T(1,128)S(1)}, f32[1,2000]{1,0:T(1,128)}, u32[]{:S(2)}) copy-start(f32[1,2000]{1,0:T(1,128)} %get-tuple-element.915) | copy-start | bytes 24004
  1554.4 2.8 copy-start.8
  1554.4 3.2 copy-start.9
  1554.4 9.3 slice-start
  1557.7 6.1 slice-start.1
  1561.7 3.2 copy-start.22
  1571.2 443.3 %copy-start.24 = (bf16[1,2,3,128,2000]{3,4,2,1,0:T(8,128)(2,1)}, bf16[1,2,3,128,2000]{3,4,2,1,0:T(8,128)(2,1)S(1)}, u32[]{:S(2)}) copy-start(bf16[1,2,3,128,2000]{3,4,2,1,0:T(8,128)(2,1)S(1)} %fusion.102) | copy-start | bytes 9216004
  (7 other events, 14.3 us)
Sparse Core Ops, SparseCore 0:
  30.1 249.0 all-reduce.13
  1553.8 456.6 all-reduce.15
where the time goes:
time: 2030 us; the launch traced here: 2020 us
  waiting for transfers between devices  698 us (34%)
  local copies, waits for them, and re-layouts  630 us (31%)
  blocking collectives  341 us (17%)
  other arithmetic  180 us (9%)
  matrix products  99.1 us (5%)
  starting transfers between devices  54.8 us (3%)
    unnamed x4, waiting for transfers between devices  676 us
    psum x3, blocking collectives, backward_layer(): lax.psum((jnp.sum(row_mask * normed_grad, axis=0), jnp.sum(row_mask * nor...  175 us
    psum x3, blocking collectives, forward_layer(): lax.psum((jnp.sum(row_mask * projected, axis=0), jnp.sum(row_mask * proje...  166 us
    slice x48, local copies, waits for them, and re-layouts, backward_layer(): lax.scan(partial(retreat_state, decay_rate), jnp.zeros((view_count, featu...  134 us
    slice x48, local copies, waits for them, and re-layouts, forward_layer(): lax.scan(partial(advance_state, decay_rate), jnp.zeros((view_count, featu...  98 us
    dynamic_update_slice x96, local copies, waits for them, and re-layouts, forward_layer(): lax.scan(partial(advance_state, decay_rate), jnp.zeros((view_count, featu...  73.3 us
    reshape x1, local copies, waits for them, and re-layouts, per_device(): weight_total.reshape(1, -1)  60.9 us
    ppermute x4, starting transfers between devices, from_behind(): return lax.ppermute(shard, axis, pairs)  54.5 us
  transfers between devices with their start and end apart: 6, of which 3 were waited for; matrix products, arithmetic and copies ran while one was open for 6% of the time, Pallas kernels for 0%

commit v1 on v0

v1 whole, which is shorter than its diff:
```python
from functools import partial

import jax
import jax.numpy as jnp
from jax import lax
from jax.experimental import pallas as pl
from jax.experimental.pallas import tpu as pltpu
from jax.sharding import PartitionSpec as P

EPSILON = 1e-05
LANES = 128
SUB = 8
HALF = SUB * LANES
COLUMNS = 256
UPPER = 96
VMEM_BYTES = 52 << 20
F32 = jnp.float32
BF16 = jnp.bfloat16
VMEM = pl.BlockSpec(memory_space=pltpu.VMEM)
SMEM = pl.BlockSpec(memory_space=pltpu.SMEM)
ANY = pl.BlockSpec(memory_space=pl.ANY)


def shaped(shape, dtype=F32):
    return jax.ShapeDtypeStruct(shape, dtype)


def params(**more):
    return pltpu.CompilerParams(vmem_limit_bytes=VMEM_BYTES, **more)


def spread_kernel(width, in_ref, out_ref):
    total = in_ref.shape[1]
    lane = lax.broadcasted_iota(jnp.int32, (in_ref.shape[0], LANES), 1)

    def aligned(q):
        low, high = q * LANES, min((q + 1) * LANES, total)
        if high - low == LANES:
            return in_ref[:, low:high].astype(F32)
        tail = jnp.zeros((in_ref.shape[0], LANES - (high - low)), F32)
        return jnp.concatenate([in_ref[:, low:high].astype(F32), tail], axis=1)

    for j in range(2 * SUB):
        q, shift = divmod(width * j, LANES)
        piece = aligned(q)
        if shift:
            piece = pltpu.roll(piece, LANES - shift, 1)
            if width > LANES - shift:
                after = pltpu.roll(aligned(q + 1), LANES - shift, 1)
                piece = jnp.where(lane < LANES - shift, piece, after)
        piece = jnp.where(lane < width, piece, 0.0).astype(out_ref.dtype)
        out_ref[j // SUB, :, (j % SUB) * LANES : (j % SUB + 1) * LANES] = piece


def spread(natural, width, rows):
    count, total = natural.shape
    return pl.pallas_call(
        partial(spread_kernel, width),
        grid=(count // rows,),
        in_specs=[pl.BlockSpec((rows, total), lambda i: (i, 0))],
        out_specs=pl.BlockSpec((2, rows, HALF), lambda i: (0, i, 0)),
        out_shape=shaped((2, count, HALF), BF16),
        compiler_params=params(),
        name="spread",
    )(natural)


def join_kernel(width, scal, own_ref, other_ref, out_ref):
    total = out_ref.shape[1]
    lane = lax.broadcasted_iota(jnp.int32, (out_ref.shape[0], LANES), 1)

    def write(halves):
        def block(j):
            at = (j % SUB) * LANES
            return halves[j // SUB][:, at : at + LANES].astype(F32)

        for q in range(pl.cdiv(total, LANES)):
            j, shift = divmod(LANES * q, width)
            piece = block(j)
            if shift:
                piece = pltpu.roll(piece, LANES - shift, 1)
            if j + 1 < 2 * SUB:
                after = pltpu.roll(block(j + 1), width - shift, 1)
                piece = jnp.where(lane < width - shift, piece, after)
            keep = min(LANES, total - q * LANES)
            out_ref[:, q * LANES : q * LANES + keep] = piece[:, :keep].astype(out_ref.dtype)

    @pl.when(scal[1] == 0)
    def _():
        write((own_ref, other_ref))

    @pl.when(scal[1] != 0)
    def _():
        write((other_ref, own_ref))


def join(scal, own, other, total, rows):
    width = total // (2 * SUB)
    count = own.shape[0]
    half = pl.BlockSpec((rows, HALF), lambda i: (i, 0))
    return pl.pallas_call(
        partial(join_kernel, width),
        grid=(count // rows,),
        in_specs=[SMEM, half, half],
        out_specs=pl.BlockSpec((rows, total), lambda i: (i, 0)),
        out_shape=shaped((count, total), own.dtype),
        compiler_params=params(),
        name="join",
    )(scal, own, other)


def load_weight(plan, layer, scal, piece_refs, weight, sems):
    copies = []
    for i, (ref_index, lead, mask, row, rows) in enumerate(plan):
        source = piece_refs[ref_index].at[(*lead, layer)]
        if mask is None:
            target = weight.at[pl.ds(row, rows), :]
        else:
            start = pl.multiple_of((scal[0] ^ mask) * LANES + row, 16)
            target = weight.at[pl.ds(start, rows), :]
        copy = pltpu.make_async_copy(source, target, sems.at[i])
        copy.start()
        copies.append(copy)
    return copies


def frame_mask(count, length):
    frame = lax.broadcasted_iota(jnp.int32, (count, 1), 0)
    return frame < length


def project_kernel(plan, layer, sizes, scal, own_ref, other_ref, *rest):
    micro, views, frames = sizes
    piece_refs, (z_ref, stats_ref, weight, sems) = rest[:-4], rest[-4:]
    for copy in load_weight(plan, layer, scal, piece_refs, weight, sems):
        copy.wait()
    sequences = micro * views
    own_at = pl.multiple_of(scal[1] * HALF, HALF)
    other_at = pl.multiple_of((1 - scal[1]) * HALF, HALF)
    for n in range(HALF // COLUMNS):
        columns = slice(n * COLUMNS, (n + 1) * COLUMNS)
        z = jnp.dot(
            own_ref[...], weight[pl.ds(own_at, HALF), columns], preferred_element_type=F32
        ) + jnp.dot(
            other_ref[...], weight[pl.ds(other_at, HALF), columns], preferred_element_type=F32
        )
        for m in range(micro):
            mask = frame_mask(frames, scal[2 + m])
            first = jnp.zeros((1, COLUMNS), F32)
            second = jnp.zeros((1, COLUMNS), F32)
            for v in range(views):
                s = m * views + v
                part = z[s * frames : (s + 1) * frames]
                kept = jnp.where(mask, part, 0.0)
                first += jnp.sum(kept, axis=0, keepdims=True)
                second += jnp.sum(kept * kept, axis=0, keepdims=True)
                for k in range(COLUMNS // LANES):
                    j = n * (COLUMNS // LANES) + k
                    z_ref[pl.ds(s * SUB + j, frames, stride=sequences * SUB), :] = part[
                        :, k * LANES : (k + 1) * LANES
                    ]
            for k in range(COLUMNS // LANES):
                j = n * (COLUMNS // LANES) + k
                for i in range(stats_ref.shape[0]):
                    stats_ref[i, m, 0, j : j + 1, :] = first[:, k * LANES : (k + 1) * LANES]
                    stats_ref[i, m, 1, j : j + 1, :] = second[:, k * LANES : (k + 1) * LANES]


def project(plan, layer, sizes, copies, scal, own, other, pieces):
    micro, views, frames = sizes
    rows = own.shape[0]
    return pl.pallas_call(
        partial(project_kernel, plan, layer, sizes),
        in_specs=[SMEM, VMEM, VMEM] + [ANY] * len(pieces),
        out_specs=[VMEM, VMEM],
        out_shape=[shaped((rows * SUB, LANES)), shaped((copies, micro, 2, SUB, LANES))],
        scratch_shapes=[
            pltpu.VMEM((2 * HALF, HALF), BF16),
            pltpu.SemaphoreType.DMA((len(plan),)),
        ],
        compiler_params=params(),
        cost_estimate=pl.CostEstimate(
            flops=4 * rows * HALF * HALF, bytes_accessed=12 * HALF * HALF, transcendentals=0
        ),
        name="project",
    )(scal, own, other, *pieces)


def normalization(stats_ref, totals, micro):
    means, inverses = [], []
    for m in range(micro):
        first = jnp.sum(stats_ref[:, m, 0], axis=0)
        second = jnp.sum(stats_ref[:, m, 1], axis=0)
        mean = first / totals[m]
        variance = second / totals[m] - mean * mean
        means.append(mean)
        inverses.append(lax.rsqrt(variance + EPSILON))
    return means, inverses


def tiled(per_micro, views):
    return jnp.concatenate([x for x in per_micro for _ in range(views)], axis=0)


def run_forward(sizes, z_ref, h_ref, slope_ref, means, inverses, par_ref):
    micro, views, frames = sizes
    step = micro * views * SUB
    gain, bias, decay = par_ref[0], par_ref[1], par_ref[2]
    scale = tiled([0.5 * gain * r for r in inverses], views)
    shift = tiled([0.5 * (bias - gain * r * mean) for mean, r in zip(means, inverses)], views)
    rate = tiled([0.5 * decay] * micro, views)
    h_ref[0:step, :] = jnp.zeros((step, LANES), F32)

    def body(t, state):
        at = pl.multiple_of(t * step, step)
        half = (z_ref[pl.ds(at, step), :] * scale + shift) + rate * state
        bent = jnp.tanh(half)
        state = half + half * bent
        h_ref[pl.ds(at + step, step), :] = state
        if slope_ref is not None:
            slope_ref[pl.ds(at, step), :] = (0.5 + 0.5 * bent) * (1.0 + half * (1.0 - bent))
        return state

    lax.fori_loop(0, frames, body, jnp.zeros((step, LANES), F32), unroll=8)


def add_residual(sizes, scal, v_ref, h_ref, y_ref):
    micro, views, frames = sizes
    step = micro * views * SUB
    for s in range(micro * views):
        mask = frame_mask(frames, scal[2 + s // views])
        for j in range(SUB):
            at = (slice(s * frames, (s + 1) * frames), slice(j * LANES, (j + 1) * LANES))
            hidden = h_ref[pl.ds(step + s * SUB + j, frames, stride=step), :]
            y = v_ref[at].astype(F32) + jnp.where(mask, hidden, 0.0)
            y_ref[at] = y.astype(BF16)


def forward_kernel(sizes, scal, totals, stats_ref, par_ref, z_ref, v_ref, y_ref, h_ref, norm_ref):
    micro = sizes[0]
    means, inverses = normalization(stats_ref, totals, micro)
    for m in range(micro):
        norm_ref[m, 0] = means[m]
        norm_ref[m, 1] = inverses[m]
    run_forward(sizes, z_ref, h_ref, None, means, inverses, par_ref)
    add_residual(sizes, scal, v_ref, h_ref, y_ref)


def forward(sizes, scal, totals, stats, par, z, v):
    micro, views, frames = sizes
    step = micro * views * SUB
    return pl.pallas_call(
        partial(forward_kernel, sizes),
        in_specs=[SMEM, SMEM, VMEM, VMEM, VMEM, VMEM],
        out_specs=[VMEM, VMEM, VMEM],
        out_shape=[
            shaped(v.shape, BF16),
            shaped(((frames + 1) * step, LANES)),
            shaped((micro, 2, SUB, LANES)),
        ],
        compiler_params=params(),
        cost_estimate=pl.CostEstimate(
            flops=8 * z.size, bytes_accessed=12 * z.size, transcendentals=z.size
        ),
        name="forward",
    )(scal, totals, stats, par, z, v)


def place_gradient(sizes, scal, s, j, value, e_ref):
    views, frames = sizes[1], sizes[2]
    step = sizes[0] * views * SUB
    mask = frame_mask(frames, scal[2 + s // views])
    e_ref[pl.ds(s * SUB + j, frames, stride=step), :] = jnp.where(mask, value, 0.0)


def run_backward(sizes, z_ref, h_ref, slope_ref, e_ref, p_ref, means, inverses, par_ref, sums_ref):
    micro, views, frames = sizes
    step = micro * views * SUB
    gain, bias, decay = par_ref[0], par_ref[1], par_ref[2]
    rate = tiled([decay] * micro, views)
    inverse = tiled(inverses, views)
    mean = tiled(means, views)
    if slope_ref is None:
        scale = tiled([0.5 * gain] * micro, views)
        shift = tiled([0.5 * bias] * micro, views)
        half_rate = 0.5 * rate
    zero = jnp.zeros((step, LANES), F32)

    def body(i, carry):
        grad, first, second, third = carry
        at = pl.multiple_of((frames - 1 - i) * step, step)
        normed = (z_ref[pl.ds(at, step), :] - mean) * inverse
        before = h_ref[pl.ds(at, step), :]
        if slope_ref is None:
            half = (normed * scale + shift) + half_rate * before
            bent = jnp.tanh(half)
            slope = (0.5 + 0.5 * bent) * (1.0 + half * (1.0 - bent))
        else:
            slope = slope_ref[pl.ds(at, step), :]
        grad = slope * (e_ref[pl.ds(at, step), :] + rate * grad)
        p_ref[pl.ds(at, step), :] = grad
        return grad, first + grad, second + grad * normed, third + grad * before

    _, *sums = lax.fori_loop(0, frames, body, (zero,) * 4, unroll=8)
    for k, total in enumerate(sums):
        for m in range(micro):
            base = m * views * SUB
            part = sum(total[base + v * SUB : base + (v + 1) * SUB] for v in range(views))
            for i in range(sums_ref.shape[0]):
                sums_ref[i, m, k] = part


def turn_kernel(
    sizes, scal, totals, stats_ref, par_ref, z_ref, v_ref, cot_ref,
    y_ref, p_ref, sums_ref, norm_ref, h_ref, slope_ref, e_ref,
):
    micro, views, frames = sizes
    means, inverses = normalization(stats_ref, totals, micro)
    for m in range(micro):
        norm_ref[m, 0] = means[m]
        norm_ref[m, 1] = inverses[m]
    for s in range(micro * views):
        for j in range(SUB):
            at = (slice(s * frames, (s + 1) * frames), slice(j * LANES, (j + 1) * LANES))
            place_gradient(sizes, scal, s, j, cot_ref[at].astype(F32), e_ref)
    run_forward(sizes, z_ref, h_ref, slope_ref, means, inverses, par_ref)
    run_backward(
        sizes, z_ref, h_ref, slope_ref, e_ref, p_ref, means, inverses, par_ref, sums_ref
    )
    add_residual(sizes, scal, v_ref, h_ref, y_ref)


def turn(sizes, copies, scal, totals, stats, par, z, v, cot):
    micro, views, frames = sizes
    step = micro * views * SUB
    return pl.pallas_call(
        partial(turn_kernel, sizes),
        in_specs=[SMEM, SMEM] + [VMEM] * 5,
        out_specs=[VMEM] * 4,
        out_shape=[
            shaped(v.shape, BF16),
            shaped(z.shape),
            shaped((copies, micro, 3, SUB, LANES)),
            shaped((micro, 2, SUB, LANES)),
        ],
        scratch_shapes=[
            pltpu.VMEM(((frames + 1) * step, LANES), F32),
            pltpu.VMEM(z.shape, F32),
            pltpu.VMEM(z.shape, F32),
        ],
        compiler_params=params(),
        cost_estimate=pl.CostEstimate(
            flops=20 * z.size, bytes_accessed=14 * z.size, transcendentals=z.size
        ),
        name="turn",
    )(scal, totals, stats, par, z, v, cot)


def backward_kernel(
    sizes, scal, par_ref, norm_ref, z_ref, h_ref, base_ref, mine_ref, theirs_ref,
    g_ref, p_ref, sums_ref, e_ref,
):
    micro, views, frames = sizes
    means = [norm_ref[m, 0] for m in range(micro)]
    inverses = [norm_ref[m, 1] for m in range(micro)]
    for s in range(micro * views):
        for j in range(SUB):
            at = (slice(s * frames, (s + 1) * frames), slice(j * LANES, (j + 1) * LANES))
            grad = base_ref[at].astype(F32) + (mine_ref[at] + theirs_ref[at])
            grad = grad.astype(BF16)
            g_ref[at] = grad
            place_gradient(sizes, scal, s, j, grad.astype(F32), e_ref)
    run_backward(sizes, z_ref, h_ref, None, e_ref, p_ref, means, inverses, par_ref, sums_ref)


def backward(sizes, copies, scal, par, norm, z, h, base, mine, theirs):
    micro = sizes[0]
    return pl.pallas_call(
        partial(backward_kernel, sizes),
        in_specs=[SMEM] + [VMEM] * 7,
        out_specs=[VMEM] * 3,
        out_shape=[
            shaped(base.shape, BF16),
            shaped(z.shape),
            shaped((copies, micro, 3, SUB, LANES)),
        ],
        scratch_shapes=[pltpu.VMEM(z.shape, F32)],
        compiler_params=params(),
        cost_estimate=pl.CostEstimate(
            flops=20 * z.size, bytes_accessed=24 * z.size, transcendentals=z.size
        ),
        name="backward",
    )(scal, par, norm, z, h, base, mine, theirs)


def unproject_kernel(plan, layer, sizes, scal, totals, sums_ref, par_ref, norm_ref, z_ref, p_ref, *rest):
    micro, views, frames = sizes
    piece_refs, (dz_ref, mine_ref, theirs_ref, weight, sems) = rest[:-5], rest[-5:]
    copies = load_weight(plan, layer, scal, piece_refs, weight, sems)
    step = micro * views * SUB
    for m in range(micro):
        first = jnp.sum(sums_ref[:, m, 0], axis=0) / totals[m]
        second = jnp.sum(sums_ref[:, m, 1], axis=0) / totals[m]
        mean, inverse = norm_ref[m, 0], norm_ref[m, 1]
        scale = inverse * par_ref[0]
        mask = frame_mask(frames, scal[2 + m])
        for v in range(views):
            s = m * views + v
            for j in range(SUB):
                row = slice(j, j + 1)
                p = p_ref[pl.ds(s * SUB + j, frames, stride=step), :]
                z = z_ref[pl.ds(s * SUB + j, frames, stride=step), :]
                normed = (z - mean[row]) * inverse[row]
                taken = jnp.where(mask, first[row] + normed * second[row], 0.0)
                dz_ref[s * frames : (s + 1) * frames, j * LANES : (j + 1) * LANES] = (
                    scale[row] * (p - taken)
                ).astype(BF16)
    for copy in copies:
        copy.wait()
    for out_ref, half in ((theirs_ref, 1 - scal[1]), (mine_ref, scal[1])):
        for n in range(HALF // COLUMNS):
            rows = pl.ds(pl.multiple_of(half * HALF + n * COLUMNS, COLUMNS), COLUMNS)
            out_ref[:, n * COLUMNS : (n + 1) * COLUMNS] = lax.dot_general(
                dz_ref[...], weight[rows, :], (((1,), (1,)), ((), ())), preferred_element_type=F32
            )


def unproject(plan, layer, sizes, scal, totals, sums, par, norm, z, p, pieces):
    rows = z.shape[0] // SUB
    return pl.pallas_call(
        partial(unproject_kernel, plan, layer, sizes),
        in_specs=[SMEM, SMEM] + [VMEM] * 5 + [ANY] * len(pieces),
        out_specs=[VMEM] * 3,
        out_shape=[shaped((rows, HALF), BF16), shaped((rows, HALF)), shaped((rows, HALF))],
        scratch_shapes=[
            pltpu.VMEM((2 * HALF, HALF), BF16),
            pltpu.SemaphoreType.DMA((len(plan),)),
        ],
        compiler_params=params(),
        cost_estimate=pl.CostEstimate(
            flops=4 * rows * HALF * HALF, bytes_accessed=24 * HALF * HALF, transcendentals=0
        ),
        name="unproject",
    )(scal, totals, sums, par, norm, z, p, *pieces)


def outer_kernel(plan, scal, own_ref, other_ref, dz_ref, *rest):
    out_refs, (grad, sems) = rest[:-2], rest[-2:]
    for v_ref, half in ((own_ref, scal[1]), (other_ref, 1 - scal[1])):
        rows = pl.ds(pl.multiple_of(half * HALF, HALF), HALF)
        for n in range(HALF // COLUMNS):
            columns = slice(n * COLUMNS, (n + 1) * COLUMNS)
            grad[rows, columns] = lax.dot_general(
                v_ref[...], dz_ref[:, columns], (((0,), (0,)), ((), ())), preferred_element_type=F32
            ).astype(grad.dtype)
    copies = []
    for i, (ref_index, lead, mask, row, count) in enumerate(plan):
        if mask is None:
            source = grad.at[pl.ds(row, count), :]
        else:
            start = pl.multiple_of((scal[0] ^ mask) * LANES + row, 16)
            source = grad.at[pl.ds(start, count), :]
        copy = pltpu.make_async_copy(source, out_refs[ref_index].at[lead], sems.at[i])
        copy.start()
        copies.append(copy)
    for copy in copies:
        copy.wait()


def outer(plan, shapes, dtype, scal, own, other, dz):
    return pl.pallas_call(
        partial(outer_kernel, plan),
        in_specs=[SMEM, VMEM, VMEM, VMEM],
        out_specs=[ANY] * len(shapes),
        out_shape=[shaped(s, dtype) for s in shapes],
        scratch_shapes=[
            pltpu.VMEM((2 * HALF, HALF), dtype),
            pltpu.SemaphoreType.DMA((len(plan),)),
        ],
        compiler_params=params(),
        cost_estimate=pl.CostEstimate(
            flops=4 * own.shape[0] * HALF * HALF, bytes_accessed=12 * HALF * HALF, transcendentals=0
        ),
        name="outer",
    )(scal, own, other, dz)


def flip(x, mask):
    count = lax.axis_size("dp")
    return lax.ppermute(x, "dp", [(i, i ^ mask) for i in range(count)])


def swap(x):
    return lax.ppermute(x, "section", [(0, 1), (1, 0)])


ROUTED = 16
FIRST = (0, 4, 1, 5, 2, 6, 3, 7)
SECOND = (8, 12, 10, 14, 9, 13, 11, 15)


def gather_pieces(shard):
    upper, lower = shard[:, :UPPER], shard[:, UPPER:]
    third = [lower] + [flip(lower, m) for m in (1, 2, 3)]
    along = [upper] + [flip(upper, m) for m in (4, 8, 12)]
    third = jnp.stack(third)
    lows = [third] + [flip(third, m) for m in (4, 8, 12)]
    a0, b0 = jnp.stack(along[:2]), jnp.stack(along[2:])
    a1, b1 = flip(a0, 1), flip(b0, 2)
    a01, b01 = jnp.concatenate([a0, a1]), jnp.concatenate([b0, b1])
    a2, b2 = flip(a01, 2), flip(b01, 1)
    pieces = [a01, a2, b01, b2] + lows
    plan = []
    for ref, masks in ((0, FIRST[:4]), (1, FIRST[4:]), (2, SECOND[:4]), (3, SECOND[4:])):
        plan += [(ref, (i,), m, 0, UPPER) for i, m in enumerate(masks)]
    for k in range(4):
        plan += [(4 + k, (i,), 4 * k + i, UPPER, LANES - UPPER) for i in range(4)]
    return pieces, plan


def scatter_plan():
    plan, shapes = [], []
    for k, masks in enumerate((FIRST[:4], FIRST[4:], SECOND[:4], SECOND[4:])):
        plan += [(k, (i,), m, 0, UPPER) for i, m in enumerate(masks)]
        shapes.append((4, UPPER, HALF))
    for k in range(4):
        plan += [(4 + k, (i,), 4 * k + i, UPPER, LANES - UPPER) for i in range(4)]
        shapes.append((4, LANES - UPPER, HALF))
    return plan, shapes


def add(*terms):
    return sum(t.astype(F32) for t in terms)


def scatter_pieces(parts):
    a01, a2, b01, b2, *lows = parts
    low = add(lows[0], *[flip(lows[k], 4 * k) for k in (1, 2, 3)]).astype(BF16)
    a01 = add(a01, flip(a2, 2)).astype(BF16)
    b01 = add(b01, flip(b2, 1)).astype(BF16)
    a0 = add(a01[:2], flip(a01[2:], 1)).astype(BF16)
    b0 = add(b01[:2], flip(b01[2:], 2)).astype(BF16)
    lower = add(low[0], *[flip(low[m], m) for m in (1, 2, 3)])
    upper = add(a0[0], flip(a0[1], 4), flip(b0[0], 8), flip(b0[1], 12))
    return jnp.concatenate([upper, lower])


def exchange(x):
    if x.shape[0] == 1:
        return lax.psum(x, "dp")
    return lax.all_to_all(x, "dp", 0, 0)


def blocks_of(matrix, width):
    matrix = matrix.reshape(2 * SUB, width, 2 * SUB, width)
    pad = LANES - width
    matrix = jnp.pad(matrix, ((0, 0), (0, pad), (0, 0), (0, pad)))
    return matrix.reshape(2 * HALF, 2, HALF).transpose(1, 0, 2)


def per_device(inputs, lengths, weights, scales, biases, decays, cotangent):
    section = lax.axis_index("section")
    group = lax.axis_index("dp")
    chips = lax.axis_size("dp")
    micro, views, frames, total = inputs.shape
    sizes = (micro, views, frames)
    rows = micro * views * frames
    width = total // (2 * SUB)
    entries = weights.shape[1]
    routed = chips == ROUTED and entries == width * total
    copies = chips if routed else 1

    own_lengths = lax.dynamic_index_in_dim(lengths, group, 1, keepdims=False)
    scal = jnp.concatenate([jnp.stack([group, section]), own_lengths]).astype(jnp.int32)
    totals = views * jnp.sum(lengths, axis=1).astype(F32)

    def both(halves, own):
        keep = lax.dynamic_index_in_dim(halves, section, 0, keepdims=False)
        got = swap(lax.dynamic_index_in_dim(halves, 1 - section, 0, keepdims=False))
        return [jnp.where(section == k, keep, got) for k in (0, 1)] if own else (keep, got)

    vectors = jnp.stack([scales[0], biases[0], decays[0]]).reshape(3, 2, SUB, width)
    vectors = jnp.pad(vectors, ((0, 0), (0, 0), (0, 0), (0, LANES - width))).transpose(1, 0, 2, 3)
    par = both(vectors, True)

    if routed:
        shard = jnp.pad(weights.reshape(width, total), ((0, LANES - width), (0, 0)))
        shard = jnp.stack(both(spread(shard, width, LANES), True))
        pieces, plan = gather_pieces(shard)
    else:
        whole = lax.all_gather(weights[0].astype(BF16), "dp", axis=0, tiled=True)
        whole = jnp.stack(both(blocks_of(whole.reshape(total, total), width), True))
        pieces, plan = [whole], [(0, (), None, 0, 2 * HALF)]

    def halves_of(x):
        spreaded = spread(x.reshape(rows, total), width, frames)
        return [lax.dynamic_index_in_dim(spreaded, k, 0, keepdims=False) for k in (section, 1 - section)]

    x_own, x_other = halves_of(inputs)
    cot_own, _ = halves_of(cotangent)

    z0, stats = project(plan, 0, sizes, copies, scal, x_own, x_other, pieces)
    y1_own, h0, norm0 = forward(sizes, scal, totals, exchange(stats), par[0], z0, x_own)
    y1_other = swap(y1_own)
    z1, stats = project(plan, 1, sizes, copies, scal, y1_own, y1_other, pieces)
    y2_own, p1, sums1, norm1 = turn(
        sizes, copies, scal, totals, exchange(stats), par[1], z1, y1_own, cot_own
    )
    sums1 = exchange(sums1)
    dz1, mine, theirs = unproject(plan, 1, sizes, scal, totals, sums1, par[1], norm1, z1, p1, pieces)
    theirs = swap(theirs)
    cut, shapes = scatter_plan() if routed else ([(0, (), None, 0, 2 * HALF)], [(2 * HALF, HALF)])
    kind = BF16 if routed else F32
    dw1 = outer(cut, shapes, kind, scal, y1_own, y1_other, dz1)
    g1_own, p0, sums0 = backward(sizes, copies, scal, par[0], norm0, z0, h0, cot_own, mine, theirs)
    sums0 = exchange(sums0)
    dz0, mine, theirs = unproject(plan, 0, sizes, scal, totals, sums0, par[0], norm0, z0, p0, pieces)
    theirs = swap(theirs)
    dw0 = outer(cut, shapes, kind, scal, x_own, x_other, dz0)
    g0_own = (g1_own.astype(F32) + (mine + theirs)).astype(BF16)

    if routed:
        grads = jnp.stack([scatter_pieces(dw0), scatter_pieces(dw1)])
        own, other = both(grads, False)[0], swap(lax.dynamic_index_in_dim(grads, 1 - section, 0, keepdims=False))
        weight_grads = join(scal, own, other, total, LANES)[:width].reshape(1, entries)
    else:
        grads = jnp.stack([dw0[0], dw1[0]])
        own, other = both(grads, False)
        square = join(scal, own, other, total, LANES).reshape(2 * SUB, LANES, total)[:, :width]
        weight_grads = lax.psum_scatter(square.reshape(1, -1), "dp", scatter_dimension=1, tiled=True)

    shape = (1, micro, views, frames, total)
    act_own = jnp.where(section == 0, y1_own, y2_own)
    act_other = jnp.where(section == 0, y1_other, swap(y2_own))
    activations = join(scal, act_own, act_other, total, frames).reshape(shape)
    grad_own = jnp.where(section == 0, g0_own, g1_own)
    grad_other = swap(jnp.where(section == 0, g1_own, g0_own))
    input_grads = join(scal, grad_own, grad_other, total, frames).reshape(shape)

    sums = [jnp.sum(s, axis=(0, 1)) for s in (sums0, sums1)]
    sums = jnp.stack(sums)[..., :width].reshape(2, 3, SUB * width)
    keep = lax.dynamic_index_in_dim(sums, section, 0, keepdims=False)
    got = swap(lax.dynamic_index_in_dim(sums, 1 - section, 0, keepdims=False))
    low = jnp.where(section == 0, keep, got)
    high = jnp.where(section == 0, got, keep)
    bias_grads, scale_grads, decay_grads = jnp.concatenate([low, high], axis=1)
    return (
        activations,
        input_grads,
        weight_grads,
        scale_grads[None],
        bias_grads[None],
        decay_grads[None],
    )


def solution(mesh):
    placed = (
        P(None, "dp", None, None),
        P(),
        P("section", "dp"),
        P("section", None),
        P("section", None),
        P("section", None),
        P(None, "dp", None, None),
    )
    return jax.shard_map(
        per_device,
        mesh=mesh,
        in_specs=placed,
        out_specs=(
            P("section", None, "dp", None, None),
            P("section", None, "dp", None, None),
            P("section", "dp"),
            P("section", None),
            P("section", None),
            P("section", None),
        ),
        check_vma=False,
    )
```

time: 2030 us -> 497 us (0.24)
  local copies, waits for them, and re-layouts: 630 us -> 39.1 us
  waiting for transfers between devices: 698 us -> 197 us
  blocking collectives: 341 us -> 16.5 us
  other arithmetic: 180 us -> 39 us
  Pallas kernels: 0 us -> 119 us
  matrix products: 99.1 us -> 0 us
  starting transfers between devices: 54.8 us -> 75.6 us
    unnamed x4 -> x0, waiting for transfers between devices: 676 us -> none
    psum x6 -> x0, blocking collectives: 341 us -> none  [the longest x3 175 us: backward_layer(): lax.psum((jnp.sum(row_mask * normed_grad, axis=0), jnp.sum(row_mask * nor...]
    slice x96 -> x4, local copies, waits for them, and re-layouts: 232 us -> 1.72 us  [the longest x2 0.87 us: scatter_pieces(): a0 = add(a01[:2], flip(a01[2:], 1)).astype(BF16)]
    ppermute x4 -> x48, waiting for transfers between devices: 21.8 us -> 195 us  [the longest x39 190 us: flip(): return lax.ppermute(x, 'dp', [(i, i ^ mask) for i in range(count)])]
    reshape x12 -> x4, local copies, waits for them, and re-layouts: 132 us -> 4.73 us  [the longest x1 3.82 us: per_device(): join(scal, own, other, total, LANES)[:width].reshape(1, entries)]
    pallas_call x0 -> x15, Pallas kernels: none -> 119 us  [the longest x2 27 us: unproject(): pl.pallas_call(partial(unproject_kernel, plan, layer, sizes), in_specs=[S...]
    dot_general x9 -> x0, matrix products: 99.1 us -> none  [the longest x3 42.1 us: backward_layer(): lax.dot_general(flat_input, proj_grad, (((0,), (0,)), ((), ())), preferre...]
    dynamic_update_slice x96 -> x0, local copies, waits for them, and re-layouts: 73.3 us -> none  [forward_layer(): lax.scan(partial(advance_state, decay_rate), jnp.zeros((view_count, featu...]
  transfers between devices with their start and end apart: 6 -> 51, of which waited for: 3 -> 27; matrix products, arithmetic and copies ran while one was open for 6% -> 12% of each run, Pallas kernels for 0% -> 13%
where the time goes in v1:
time: 497 us; the launch traced here: 488 us
  waiting for transfers between devices  197 us (40%)
  Pallas kernels  119 us (24%)
  starting transfers between devices  75.6 us (15%)
  local copies, waits for them, and re-layouts  39.1 us (8%)
  other arithmetic  39 us (8%)
  blocking collectives  16.5 us (3%)
    ppermute x39, waiting for transfers between devices, flip(): return lax.ppermute(x, 'dp', [(i, i ^ mask) for i in range(count)])  190 us
    ppermute x39, starting transfers between devices, flip(): return lax.ppermute(x, 'dp', [(i, i ^ mask) for i in range(count)])  33.4 us
    pallas_call x2, Pallas kernels, unproject(): pl.pallas_call(partial(unproject_kernel, plan, layer, sizes), in_specs=[S...  27 us
    unnamed x79, local copies, waits for them, and re-layouts  23.7 us
    ppermute x9, starting transfers between devices, swap(): return lax.ppermute(x, 'section', [(0, 1), (1, 0)])  23.5 us
    pallas_call x2, Pallas kernels, project(): pl.pallas_call(partial(project_kernel, plan, layer, sizes), in_specs=[SME...  20.9 us
    all_to_all x3, starting transfers between devices, exchange(): return lax.all_to_all(x, 'dp', 0, 0)  18.6 us
    pallas_call x2, Pallas kernels, outer(): pl.pallas_call(partial(outer_kernel, plan), in_specs=[SMEM, VMEM, VMEM, V...  17.7 us
  transfers between devices with their start and end apart: 51, of which 27 were waited for; matrix products, arithmetic and copies ran while one was open for 12% of the time, Pallas kernels for 13%

profile of v1, /device:TPU:19, one launch (start us, length us, event | category | flops | bytes accessed | tf_op | source)
XLA Modules:
  0.0 488.4 jit_solution(9049146370583715969)
XLA Ops:
  0.6 11.4 %reduce.1 = f32[250000]{0:T(1024)S(1)} reduce(f32[1,250000]{1,0:T(1,128)} %param.9, f32[]{:T(128)} %constant.69), dimensions={0}, to_apply=%param.9.reduce_sub_computation | reduce | bytes 2000004 | tf_op args[2]
  18.8 21.5 %collective-permute-done.4 = bf16[2,96,1024]{2,1,0:T(8,128)(2,1)S(1)} collective-permute-done((bf16[2,96,1024]{2,1,0:T(8,128)(2,1)S(1)}, bf16[2,96,1024]{2,1,0:T(8,128)(2,1)S(1)}, u32[]{:S(2)}, u32[]{:S(2)}) %collective-permute-start.4) | collective-permute-done | bytes 393248 | tf_op jit(solution)/shard_map/ppermute | solution.py:490
  40.3 12.2 %collective-permute-done.5 = bf16[2,96,1024]{2,1,0:T(8,128)(2,1)S(1)} collective-permute-done((bf16[2,96,1024]{2,1,0:T(8,128)(2,1)S(1)}, bf16[2,96,1024]{2,1,0:T(8,128)(2,1)S(1)}, u32[]{:S(2)}, u32[]{:S(2)}) %collective-permute-start.5) | collective-permute-done | bytes 393248 | tf_op jit(solution)/shard_map/ppermute | solution.py:490
  54.4 16.9 %collective-permute-done.6 = bf16[2,2,96,1024]{3,2,1,0:T(8,128)(2,1)S(1)} collective-permute-done((bf16[2,2,96,1024]{3,2,1,0:T(8,128)(2,1)S(1)}, bf16[2,2,96,1024]{3,2,1,0:T(8,128)(2,1)S(1)}, u32[]{:S(2)}, u32[]{:S(2)}) %collective-permute-start.6) | collective-permute-done | bytes 786464 | tf_op jit(solution)/shard_map/ppermute | solution.py:490
  77.1 4.7 copy.18
  81.8 6.0 %spread.3 = bf16[2,768,1024]{2,1,0:T(8,128)(2,1)} custom-call(bf16[768,2000]{1,0:T(8,128)(2,1)} %bitcast.110), custom_call_target="tpu_custom_call" | custom-call | tf_op jit(solution)/shard_map/spread/pallas_call | solution.py:57
  87.9 21.2 %collective-permute-done.8 = bf16[2,32,1024]{2,1,0:T(8,128)(2,1)S(1)} collective-permute-done((bf16[2,32,1024]{2,1,0:T(8,128)(2,1)S(1)}, bf16[2,32,1024]{2,1,0:T(8,128)(2,1)S(1)}, u32[]{:S(2)}, u32[]{:S(2)}) %collective-permute-start.8) | collective-permute-done | bytes 131104 | tf_op jit(solution)/shard_map/ppermute | solution.py:490
  109.0 3.2 collective-permute-done.9
  115.6 3.9 dynamic-slice_bitcast_fusion.1
  119.5 10.0 %collective-permute-done.11.rest_5_ = bf16[4,2,32,1024]{3,2,1,0:T(8,128)(2,1)S(1)} collective-permute-done((bf16[4,2,32,1024]{3,2,1,0:T(8,128)(2,1)S(1)}, bf16[4,2,32,1024]{3,2,1,0:T(8,128)(2,1)S(1)}, u32[]{:S(2)}, u32[]{:S(2)}) %collective-permute-start.11) | collective-permute-done | bytes 524320 | tf_op jit(solution)/shard_map/ppermute | solution.py:490
  132.2 24.7 %collective-permute-done.13.rest_7_ = bf16[4,2,32,1024]{3,2,1,0:T(8,128)(2,1)} collective-permute-done((bf16[4,2,32,1024]{3,2,1,0:T(8,128)(2,1)S(1)}, bf16[4,2,32,1024]{3,2,1,0:T(8,128)(2,1)}, u32[]{:S(2)}, u32[]{:S(2)}) %collective-permute-start.13) | collective-permute-done | bytes 524320 | tf_op jit(solution)/shard_map/ppermute | solution.py:490
  156.9 10.5 %project.2 = (f32[6144,128]{1,0:T(8,128)}, f32[16,2,2,8,128]{4,3,2,1,0:T(8,128)}) custom-call(s32[4]{0:T(128)S(1)} %pad_add_fusion.scal, bf16[768,1024]{1,0:T(8,128)(2,1)} %get-tuple-element.93.own_ref.v_ref, bf16[768,1024]{1,0:T(8,128)(2,1)} %get-tuple-element.92.other_ref, bf16[4,2,96,1024]{3,2,1,0:T(8,128)(2,1)} %pad_maximum_fusion.rest_0_, ...), custom_call_target="tpu_custom_call" | custom-call | flops 3221225472 | bytes 12582912 | tf_op jit(solution)/shard_map/project/pallas_call | solution.py:172
  167.4 8.0 %all-to-all-start = ((f32[16,2,2,8,128]{4,3,2,1,0:T(8,128)}), f32[16,2,2,8,128]{4,3,2,1,0:T(8,128)S(1)}, u32[]{:S(2)}, u32[]{:S(2)}) async-start(f32[16,2,2,8,128]{4,3,2,1,0:T(8,128)} %get-tuple-element.42), calls=%async_computation | async-start | bytes 524288 | tf_op jit(solution)/shard_map/all_to_all | solution.py:551
  175.4 4.2 collective-permute-start.14
  180.5 5.4 %forward.1 = (bf16[768,1024]{1,0:T(8,128)(2,1)S(1)}, f32[6192,128]{1,0:T(8,128)}, f32[2,2,8,128]{3,2,1,0:T(8,128)S(1)}) custom-call(s32[4]{0:T(128)S(1)} %pad_add_fusion.scal, f32[2]{0:T(128)S(1)} %convert_multiply_fusion.totals, f32[16,2,2,8,128]{4,3,2,1,0:T(8,128)S(1)} %all-to-all-done.stats_ref, f32[3,8,128]{2,1,0:T(8,128)S(1)} %get-tuple-element.109.par_ref, ...), custom_call_target="tpu_custom_call" | custom-call | flops 6291456 | bytes 9437184 | tf_op jit(solution)/shard_map/forward/pallas_call | solution.py:252
  186.0 5.0 %collective-permute-start.15 = (bf16[768,1024]{1,0:T(8,128)(2,1)S(1)}, bf16[768,1024]{1,0:T(8,128)(2,1)S(1)}, u32[]{:S(2)}, u32[]{:S(2)}) collective-permute-start(bf16[768,1024]{1,0:T(8,128)(2,1)S(1)} %get-tuple-element.44.own_ref.v_ref), channel_id=1, source_target_pairs={{0,16},{16,0},{1,17},{17,1},{2,18},{18,2},{3,19},{19,3},{4,20},{20... | collective-permute-start | bytes 4718600 | tf_op jit(solution)/shard_map/ppermute | solution.py:494
  191.0 3.0 collective-permute-done.15.other_ref
  195.2 10.4 %project.3 = (f32[6144,128]{1,0:T(8,128)}, f32[16,2,2,8,128]{4,3,2,1,0:T(8,128)}) custom-call(s32[4]{0:T(128)S(1)} %pad_add_fusion.scal, bf16[768,1024]{1,0:T(8,128)(2,1)} %copy-done, bf16[768,1024]{1,0:T(8,128)(2,1)} %copy-done.20, bf16[4,2,96,1024]{3,2,1,0:T(8,128)(2,1)} %pad_maximum_fusion.rest_0_, ...), custom_call_target="tpu_custom_call" | custom-call | flops 3221225472 | bytes 12582912 | tf_op jit(solution)/shard_map/project/pallas_call | solution.py:172
  205.6 5.7 %all-to-all-start.1 = ((f32[16,2,2,8,128]{4,3,2,1,0:T(8,128)}), f32[16,2,2,8,128]{4,3,2,1,0:T(8,128)S(1)}, u32[]{:S(2)}, u32[]{:S(2)}) async-start(f32[16,2,2,8,128]{4,3,2,1,0:T(8,128)} %get-tuple-element.45), calls=%async_computation.1 | async-start | bytes 524288 | tf_op jit(solution)/shard_map/all_to_all | solution.py:551
  211.2 4.7 copy.20
  216.0 6.0 %spread.5 = bf16[2,768,1024]{2,1,0:T(8,128)(2,1)} custom-call(bf16[768,2000]{1,0:T(8,128)(2,1)} %bitcast.111), custom_call_target="tpu_custom_call" | custom-call | tf_op jit(solution)/shard_map/spread/pallas_call | solution.py:57
  224.7 10.1 %turn.1 = (bf16[768,1024]{1,0:T(8,128)(2,1)}, f32[6144,128]{1,0:T(8,128)}, f32[16,2,3,8,128]{4,3,2,1,0:T(8,128)S(1)}, f32[2,2,8,128]{3,2,1,0:T(8,128)S(1)}) custom-call(s32[4]{0:T(128)S(1)} %pad_add_fusion.scal, f32[2]{0:T(128)S(1)} %convert_multiply_fusion.totals, f32[16,2,2,8,128]{4,3,2,1,0:T(8,128)S(1)} %all-to-all-done.1.stats_ref, ...), custom_call_target="tpu_custom_call" | custom-call | flops 15728640 | bytes 11010048 | tf_op jit(solution)/shard_map/turn/pallas_call | solution.py:336
  234.8 16.5 %all_to_all.20.sums_ref = f32[16,2,3,8,128]{4,3,2,1,0:T(8,128)S(1)} all-to-all(f32[16,2,3,8,128]{4,3,2,1,0:T(8,128)S(1)} %get-tuple-element.50), channel_id=1, replica_groups=mesh['section'=2,'dp'=16] {'dp'}, dimensions={0} | all-to-all | bytes 786432 | tf_op jit(solution)/shard_map/all_to_all | solution.py:551
  251.3 13.4 %unproject.2 = (bf16[768,1024]{1,0:T(8,128)(2,1)}, f32[768,1024]{1,0:T(8,128)}, f32[768,1024]{1,0:T(8,128)}) custom-call(s32[4]{0:T(128)S(1)} %pad_add_fusion.scal, f32[2]{0:T(128)S(1)} %convert_multiply_fusion.totals, f32[16,2,3,8,128]{4,3,2,1,0:T(8,128)S(1)} %all_to_all.20.sums_ref, f32[3,8,128]{2,1,0:T(8,128)S(1)} %get-tuple-element.108.par_ref, ...), custom_call_target="tpu_custom_call" | custom-call | flops 3221225472 | bytes 25165824 | tf_op jit(solution)/shard_map/unproject/pallas_call | solution.py:430
  266.0 8.8 %outer.3 = (bf16[4,96,1024]{2,1,0:T(8,128)(2,1)S(1)}, bf16[4,96,1024]{2,1,0:T(8,128)(2,1)}, bf16[4,96,1024]{2,1,0:T(8,128)(2,1)}, bf16[4,96,1024]{2,1,0:T(8,128)...) custom-call(s32[4]{0:T(128)S(1)} %pad_add_fusion.scal, ...), custom_call_target="tpu_custom_call" | custom-call | flops 3221225472 | bytes 12582912 | tf_op jit(solution)/shard_map/outer/pallas_call | solution.py:471
  278.7 6.1 %collective-permute-done.40 = bf16[4,32,1024]{2,1,0:T(8,128)(2,1)S(1)} collective-permute-done((bf16[4,32,1024]{2,1,0:T(8,128)(2,1)S(1)}, bf16[4,32,1024]{2,1,0:T(8,128)(2,1)S(1)}, u32[]{:S(2)}, u32[]{:S(2)}) %collective-permute-start.40) | collective-permute-done | bytes 262176 | tf_op jit(solution)/shard_map/ppermute | solution.py:490
  286.3 8.8 %collective-permute-done.41 = bf16[4,32,1024]{2,1,0:T(8,128)(2,1)} collective-permute-done((bf16[4,32,1024]{2,1,0:T(8,128)(2,1)}, bf16[4,32,1024]{2,1,0:T(8,128)(2,1)}, u32[]{:S(2)}, u32[]{:S(2)}) %collective-permute-start.41) | collective-permute-done | bytes 262176 | tf_op jit(solution)/shard_map/ppermute | solution.py:490
  295.1 6.7 %collective-permute-done.42 = bf16[4,32,1024]{2,1,0:T(8,128)(2,1)} collective-permute-done((bf16[4,32,1024]{2,1,0:T(8,128)(2,1)S(1)}, bf16[4,32,1024]{2,1,0:T(8,128)(2,1)}, u32[]{:S(2)}, u32[]{:S(2)}) %collective-permute-start.42) | collective-permute-done | bytes 262176 | tf_op jit(solution)/shard_map/ppermute | solution.py:490
  312.5 11.9 %backward.1 = (bf16[768,1024]{1,0:T(8,128)(2,1)S(1)}, f32[6144,128]{1,0:T(8,128)}, f32[16,2,3,8,128]{4,3,2,1,0:T(8,128)}) custom-call(s32[4]{0:T(128)S(1)} %pad_add_fusion.scal, f32[3,8,128]{2,1,0:T(8,128)S(1)} %get-tuple-element.109.par_ref, f32[2,2,8,128]{3,2,1,0:T(8,128)S(1)} %get-tuple-element.48.norm_ref, f32[6144,128]{1,0:T(8,128)} %get-tuple-element.43.z_ref, ...), custom_call_target="tpu_custom_call" | custom-call | flops 15728640 | bytes 18874368 | tf_op jit(solution)/shard_map/backward/pallas_call | solution.py:378
  325.5 5.0 %all-to-all-start.3 = ((f32[16,2,3,8,128]{4,3,2,1,0:T(8,128)}), f32[16,2,3,8,128]{4,3,2,1,0:T(8,128)S(1)}, u32[]{:S(2)}, u32[]{:S(2)}) async-start(f32[16,2,3,8,128]{4,3,2,1,0:T(8,128)} %get-tuple-element.56), calls=%async_computation.3 | async-start | bytes 786432 | tf_op jit(solution)/shard_map/all_to_all | solution.py:551
  339.2 13.6 %unproject.3 = (bf16[768,1024]{1,0:T(8,128)(2,1)}, f32[768,1024]{1,0:T(8,128)}, f32[768,1024]{1,0:T(8,128)}) custom-call(s32[4]{0:T(128)S(1)} %pad_add_fusion.scal, f32[2]{0:T(128)S(1)} %copy-done.14, f32[16,2,3,8,128]{4,3,2,1,0:T(8,128)S(1)} %all-to-all-done.3.sums_ref, f32[3,8,128]{2,1,0:T(8,128)S(1)} %get-tuple-element.109.par_ref, ...), custom_call_target="tpu_custom_call" | custom-call | flops 3221225472 | bytes 25165824 | tf_op jit(solution)/shard_map/unproject/pallas_call | solution.py:430
  352.8 4.5 collective-permute-start.18
  357.3 8.9 %outer.2 = (bf16[4,96,1024]{2,1,0:T(8,128)(2,1)S(1)}, bf16[4,96,1024]{2,1,0:T(8,128)(2,1)}, bf16[4,96,1024]{2,1,0:T(8,128)(2,1)}, bf16[4,96,1024]{2,1,0:T(8,128)...) custom-call(s32[4]{0:T(128)S(1)} %pad_add_fusion.scal, ...), custom_call_target="tpu_custom_call" | custom-call | flops 3221225472 | bytes 12582912 | tf_op jit(solution)/shard_map/outer/pallas_call | solution.py:471
  366.3 2.8 collective-permute-start.38
  371.8 9.2 %collective-permute-done.38 = bf16[96,1024]{1,0:T(8,128)(2,1)S(1)} collective-permute-done((bf16[96,1024]{1,0:T(8,128)(2,1)S(1)}, bf16[96,1024]{1,0:T(8,128)(2,1)S(1)}, u32[]{:S(2)}, u32[]{:S(2)}) %collective-permute-start.38) | collective-permute-done | bytes 196640 | tf_op jit(solution)/shard_map/ppermute | solution.py:490
  381.0 5.0 %collective-permute-done.39 = bf16[96,1024]{1,0:T(8,128)(2,1)S(1)} collective-permute-done((bf16[96,1024]{1,0:T(8,128)(2,1)S(1)}, bf16[96,1024]{1,0:T(8,128)(2,1)S(1)}, u32[]{:S(2)}, u32[]{:S(2)}) %collective-permute-start.39) | collective-permute-done | bytes 196640 | tf_op jit(solution)/shard_map/ppermute | solution.py:490
  393.4 11.1 %collective-permute-done.28 = bf16[4,32,1024]{2,1,0:T(8,128)(2,1)} collective-permute-done((bf16[4,32,1024]{2,1,0:T(8,128)(2,1)S(1)}, bf16[4,32,1024]{2,1,0:T(8,128)(2,1)}, u32[]{:S(2)}, u32[]{:S(2)}) %collective-permute-start.28) | collective-permute-done | bytes 262176 | tf_op jit(solution)/shard_map/ppermute | solution.py:490
  407.3 5.6 %collective-permute-done.29 = bf16[4,32,1024]{2,1,0:T(8,128)(2,1)} collective-permute-done((bf16[4,32,1024]{2,1,0:T(8,128)(2,1)S(1)}, bf16[4,32,1024]{2,1,0:T(8,128)(2,1)}, u32[]{:S(2)}, u32[]{:S(2)}) %collective-permute-start.29) | collective-permute-done | bytes 262176 | tf_op jit(solution)/shard_map/ppermute | solution.py:490
  419.1 6.2 %collective-permute-done.21 = bf16[2,96,1024]{2,1,0:T(8,128)(2,1)S(1)} collective-permute-done((bf16[2,96,1024]{2,1,0:T(8,128)(2,1)S(1)}, bf16[2,96,1024]{2,1,0:T(8,128)(2,1)S(1)}, u32[]{:S(2)}, u32[]{:S(2)}) %collective-permute-start.21) | collective-permute-done | bytes 393248 | tf_op jit(solution)/shard_map/ppermute | solution.py:490
  428.0 4.2 broadcast_select_fusion
  432.2 3.5 collective-permute-start.19
  438.4 5.0 %collective-permute-done.22 = bf16[96,1024]{1,0:T(8,128)(2,1)S(1)} collective-permute-done((bf16[96,1024]{1,0:T(8,128)(2,1)S(1)}, bf16[96,1024]{1,0:T(8,128)(2,1)S(1)}, u32[]{:S(2)}, u32[]{:S(2)}) %collective-permute-start.22) | collective-permute-done | bytes 196640 | tf_op jit(solution)/shard_map/ppermute | solution.py:490
  446.6 9.2 %collective-permute-done.26 = bf16[96,1024]{1,0:T(8,128)(2,1)S(1)} collective-permute-done((bf16[96,1024]{1,0:T(8,128)(2,1)S(1)}, bf16[96,1024]{1,0:T(8,128)(2,1)S(1)}, u32[]{:S(2)}, u32[]{:S(2)}) %collective-permute-start.26) | collective-permute-done | bytes 196640 | tf_op jit(solution)/shard_map/ppermute | solution.py:490
  459.6 5.7 %join.3 = bf16[768,2000]{1,0:T(8,128)(2,1)} custom-call(s32[4]{0:T(128)S(1)} %pad_add_fusion.scal, bf16[768,1024]{1,0:T(8,128)(2,1)S(1)} %broadcast_select_fusion.3.own_ref, bf16[768,1024]{1,0:T(8,128)(2,1)} %broadcast_select_fusion.2.other_ref), custom_call_target="tpu_custom_call" | custom-call | tf_op jit(solution)/shard_map/join/pallas_call | solution.py:101
  465.3 4.7 copy.21
  474.0 3.8 reshape.54
  477.8 5.7 %join.4 = bf16[768,2000]{1,0:T(8,128)(2,1)} custom-call(s32[4]{0:T(128)S(1)} %pad_add_fusion.scal, bf16[768,1024]{1,0:T(8,128)(2,1)S(1)} %get-tuple-element.91.own_ref, bf16[768,1024]{1,0:T(8,128)(2,1)} %collective-permute-done.19.other_ref), custom_call_target="tpu_custom_call" | custom-call | tf_op jit(solution)/shard_map/join/pallas_call | solution.py:101
  483.6 4.6 copy.22
  (211 shorter events, 87.7 us)
Async XLA Ops:
  15.2 25.1 %collective-permute-start.4 = (bf16[2,96,1024]{2,1,0:T(8,128)(2,1)S(1)}, bf16[2,96,1024]{2,1,0:T(8,128)(2,1)S(1)}, u32[]{:S(2)}, u32[]{:S(2)}) collective-permute-start(bf16[2,96,1024]{2,1,0:T(8,128)(2,1)S(1)} %fusion.4), channel_id=1, source_target_pairs={{0,8},{1,9},{2,10},{3,11},{4,12},{5,13},{6,14},{7,15},{8,0},{9,1},... | collective-permute-start | bytes 1179656 | tf_op jit(solution)/shard_map/ppermute | solution.py:490
  15.3 37.2 %collective-permute-start.5 = (bf16[2,96,1024]{2,1,0:T(8,128)(2,1)S(1)}, bf16[2,96,1024]{2,1,0:T(8,128)(2,1)S(1)}, u32[]{:S(2)}, u32[]{:S(2)}) collective-permute-start(bf16[2,96,1024]{2,1,0:T(8,128)(2,1)S(1)} %fusion.4), channel_id=1, source_target_pairs={{0,12},{1,13},{2,14},{3,15},{4,8},{5,9},{6,10},{7,11},{8,4},{9,5},... | collective-permute-start | bytes 1179656 | tf_op jit(solution)/shard_map/ppermute | solution.py:490
  17.7 36.2 %collective-permute-start.1 = (bf16[2,96,1024]{2,1,0:T(8,128)(2,1)S(1)}, bf16[2,96,1024]{2,1,0:T(8,128)(2,1)S(1)}, u32[]{:S(2)}, u32[]{:S(2)}) collective-permute-start(bf16[2,96,1024]{2,1,0:T(8,128)(2,1)S(1)} %fusion.4), channel_id=1, source_target_pairs={{0,4},{1,5},{2,6},{3,7},{4,0},{5,1},{6,2},{7,3},{8,12},{9,13},{10,... | collective-permute-start | bytes 1179656 | tf_op jit(solution)/shard_map/ppermute | solution.py:490
  52.6 18.7 %collective-permute-start.6 = (bf16[2,2,96,1024]{3,2,1,0:T(8,128)(2,1)S(1)}, bf16[2,2,96,1024]{3,2,1,0:T(8,128)(2,1)S(1)}, u32[]{:S(2)}, u32[]{:S(2)}) collective-permute-start(bf16[2,2,96,1024]{3,2,1,0:T(8,128)(2,1)S(1)} %pad_maximum_fusion.3), channel_id=1, source_target_pairs={{0,2},{1,3},{2,0},{3,1},{4,6},{5,7},{6,4},{7,5},{8,10},{9,11},{10,... | collective-permute-start | bytes 2359304 | tf_op jit(solution)/shard_map/ppermute | solution.py:490
  54.0 18.4 %collective-permute-start.2 = (bf16[2,2,96,1024]{3,2,1,0:T(8,128)(2,1)S(1)}, bf16[2,2,96,1024]{3,2,1,0:T(8,128)(2,1)S(1)}, u32[]{:S(2)}, u32[]{:S(2)}) collective-permute-start(bf16[2,2,96,1024]{3,2,1,0:T(8,128)(2,1)S(1)} %pad_maximum_fusion.2), channel_id=1, source_target_pairs={{0,1},{1,0},{2,3},{3,2},{4,5},{5,4},{6,7},{7,6},{8,9},{9,8},{10,11... | collective-permute-start | bytes 2359304 | tf_op jit(solution)/shard_map/ppermute | solution.py:490
  71.5 85.4 %collective-permute-start.7 = (bf16[4,2,96,1024]{3,2,1,0:T(8,128)(2,1)S(1)}, bf16[4,2,96,1024]{3,2,1,0:T(8,128)(2,1)}, u32[]{:S(2)}, u32[]{:S(2)}) collective-permute-start(bf16[4,2,96,1024]{3,2,1,0:T(8,128)(2,1)S(1)} %pad_maximum_fusion.1.rest_2_), channel_id=1, source_target_pairs={{0,1},{1,0},{2,3},{3,2},{4,5},{5,4},{6,7},{7,6},{8,9},{9,8},{10,11... | collective-permute-start | bytes 4718600 | tf_op jit(solution)/shard_map/ppermute | solution.py:490
  73.7 83.1 %collective-permute-start.3 = (bf16[4,2,96,1024]{3,2,1,0:T(8,128)(2,1)}, bf16[4,2,96,1024]{3,2,1,0:T(8,128)(2,1)}, u32[]{:S(2)}, u32[]{:S(2)}) collective-permute-start(bf16[4,2,96,1024]{3,2,1,0:T(8,128)(2,1)} %pad_maximum_fusion.rest_0_), channel_id=1, source_target_pairs={{0,2},{1,3},{2,0},{3,1},{4,6},{5,7},{6,4},{7,5},{8,10},{9,11},{10,... | collective-permute-start | bytes 4718600 | tf_op jit(solution)/shard_map/ppermute | solution.py:490
  74.4 34.6 %collective-permute-start.8 = (bf16[2,32,1024]{2,1,0:T(8,128)(2,1)S(1)}, bf16[2,32,1024]{2,1,0:T(8,128)(2,1)S(1)}, u32[]{:S(2)}, u32[]{:S(2)}) collective-permute-start(bf16[2,32,1024]{2,1,0:T(8,128)(2,1)S(1)} %pad_maximum_fusion.5), channel_id=1, source_target_pairs={{0,1},{1,0},{2,3},{3,2},{4,5},{5,4},{6,7},{7,6},{8,9},{9,8},{10,11... | collective-permute-start | bytes 393224 | tf_op jit(solution)/shard_map/ppermute | solution.py:490
  75.6 36.6 %collective-permute-start.9 = (bf16[2,32,1024]{2,1,0:T(8,128)(2,1)S(1)}, bf16[2,32,1024]{2,1,0:T(8,128)(2,1)S(1)}, u32[]{:S(2)}, u32[]{:S(2)}) collective-permute-start(bf16[2,32,1024]{2,1,0:T(8,128)(2,1)S(1)} %pad_maximum_fusion.5), channel_id=1, source_target_pairs={{0,2},{1,3},{2,0},{3,1},{4,6},{5,7},{6,4},{7,5},{8,10},{9,11},{10,... | collective-permute-start | bytes 393224 | tf_op jit(solution)/shard_map/ppermute | solution.py:490
  75.9 36.5 %collective-permute-start.10 = (bf16[2,32,1024]{2,1,0:T(8,128)(2,1)S(1)}, bf16[2,32,1024]{2,1,0:T(8,128)(2,1)S(1)}, u32[]{:S(2)}, u32[]{:S(2)}) collective-permute-start(bf16[2,32,1024]{2,1,0:T(8,128)(2,1)S(1)} %pad_maximum_fusion.5), channel_id=1, source_target_pairs={{0,3},{1,2},{2,1},{3,0},{4,7},{5,6},{6,5},{7,4},{8,11},{9,10},{10,... | collective-permute-start | bytes 393224 | tf_op jit(solution)/shard_map/ppermute | solution.py:490
  112.5 17.0 %collective-permute-start.11 = (bf16[4,2,32,1024]{3,2,1,0:T(8,128)(2,1)S(1)}, bf16[4,2,32,1024]{3,2,1,0:T(8,128)(2,1)S(1)}, u32[]{:S(2)}, u32[]{:S(2)}) collective-permute-start(bf16[4,2,32,1024]{3,2,1,0:T(8,128)(2,1)S(1)} %pad_maximum_fusion.4.rest_4_), channel_id=1, source_target_pairs={{0,4},{1,5},{2,6},{3,7},{4,0},{5,1},{6,2},{7,3},{8,12},{9,13},{10,... | collective-permute-start | bytes 1572872 | tf_op jit(solution)/shard_map/ppermute | solution.py:490
  112.5 19.7 %collective-permute-start.12 = (bf16[4,2,32,1024]{3,2,1,0:T(8,128)(2,1)S(1)}, bf16[4,2,32,1024]{3,2,1,0:T(8,128)(2,1)S(1)}, u32[]{:S(2)}, u32[]{:S(2)}) collective-permute-start(bf16[4,2,32,1024]{3,2,1,0:T(8,128)(2,1)S(1)} %pad_maximum_fusion.4.rest_4_), channel_id=1, source_target_pairs={{0,8},{1,9},{2,10},{3,11},{4,12},{5,13},{6,14},{7,15},{8,0},{9,1},... | collective-permute-start | bytes 1572872 | tf_op jit(solution)/shard_map/ppermute | solution.py:490
  113.0 43.9 %collective-permute-start.13 = (bf16[4,2,32,1024]{3,2,1,0:T(8,128)(2,1)S(1)}, bf16[4,2,32,1024]{3,2,1,0:T(8,128)(2,1)}, u32[]{:S(2)}, u32[]{:S(2)}) collective-permute-start(bf16[4,2,32,1024]{3,2,1,0:T(8,128)(2,1)S(1)} %pad_maximum_fusion.4.rest_4_), channel_id=1, source_target_pairs={{0,12},{1,13},{2,14},{3,15},{4,8},{5,9},{6,10},{7,11},{8,4},{9,5},... | collective-permute-start | bytes 1572872 | tf_op jit(solution)/shard_map/ppermute | solution.py:490
  167.4 13.1 %all-to-all-start = ((f32[16,2,2,8,128]{4,3,2,1,0:T(8,128)}), f32[16,2,2,8,128]{4,3,2,1,0:T(8,128)S(1)}, u32[]{:S(2)}, u32[]{:S(2)}) async-start(f32[16,2,2,8,128]{4,3,2,1,0:T(8,128)} %get-tuple-element.42), calls=%async_computation | async-start | bytes 524288 | tf_op jit(solution)/shard_map/all_to_all | solution.py:551
  186.0 8.1 %collective-permute-start.15 = (bf16[768,1024]{1,0:T(8,128)(2,1)S(1)}, bf16[768,1024]{1,0:T(8,128)(2,1)S(1)}, u32[]{:S(2)}, u32[]{:S(2)}) collective-permute-start(bf16[768,1024]{1,0:T(8,128)(2,1)S(1)} %get-tuple-element.44.own_ref.v_ref), channel_id=1, source_target_pairs={{0,16},{16,0},{1,17},{17,1},{2,18},{18,2},{3,19},{19,3},{4,20},{20... | collective-permute-start | bytes 4718600 | tf_op jit(solution)/shard_map/ppermute | solution.py:494
  205.6 19.1 %all-to-all-start.1 = ((f32[16,2,2,8,128]{4,3,2,1,0:T(8,128)}), f32[16,2,2,8,128]{4,3,2,1,0:T(8,128)S(1)}, u32[]{:S(2)}, u32[]{:S(2)}) async-start(f32[16,2,2,8,128]{4,3,2,1,0:T(8,128)} %get-tuple-element.45), calls=%async_computation.1 | async-start | bytes 524288 | tf_op jit(solution)/shard_map/all_to_all | solution.py:551
  264.8 46.7 %collective-permute-start.17 = (f32[768,1024]{1,0:T(8,128)}, f32[768,1024]{1,0:T(8,128)}, u32[]{:S(2)}, u32[]{:S(2)}) collective-permute-start(f32[768,1024]{1,0:T(8,128)} %get-tuple-element.54), channel_id=1, source_target_pairs={{0,16},{16,0},{1,17},{17,1},{2,18},{18,2},{3,19},{19,3},{4,20},{20... | collective-permute-start | bytes 9437192 | tf_op jit(solution)/shard_map/ppermute | solution.py:494
  274.7 10.0 %collective-permute-start.40 = (bf16[4,32,1024]{2,1,0:T(8,128)(2,1)S(1)}, bf16[4,32,1024]{2,1,0:T(8,128)(2,1)S(1)}, u32[]{:S(2)}, u32[]{:S(2)}) collective-permute-start(bf16[4,32,1024]{2,1,0:T(8,128)(2,1)S(1)} %get-tuple-element.75), channel_id=1, source_target_pairs={{0,4},{1,5},{2,6},{3,7},{4,0},{5,1},{6,2},{7,3},{8,12},{9,13},{10,... | collective-permute-start | bytes 786440 | tf_op jit(solution)/shard_map/ppermute | solution.py:490
  275.3 27.7 %collective-permute-start.33 = (bf16[4,96,1024]{2,1,0:T(8,128)(2,1)}, bf16[4,96,1024]{2,1,0:T(8,128)(2,1)}, u32[]{:S(2)}, u32[]{:S(2)}) collective-permute-start(bf16[4,96,1024]{2,1,0:T(8,128)(2,1)} %get-tuple-element.71), channel_id=1, source_target_pairs={{0,2},{1,3},{2,0},{3,1},{4,6},{5,7},{6,4},{7,5},{8,10},{9,11},{10,... | collective-permute-start | bytes 2359304 | tf_op jit(solution)/shard_map/ppermute | solution.py:490
  276.3 31.7 %collective-permute-start.36 = (bf16[4,96,1024]{2,1,0:T(8,128)(2,1)}, bf16[4,96,1024]{2,1,0:T(8,128)(2,1)}, u32[]{:S(2)}, u32[]{:S(2)}) collective-permute-start(bf16[4,96,1024]{2,1,0:T(8,128)(2,1)} %get-tuple-element.73), channel_id=1, source_target_pairs={{0,1},{1,0},{2,3},{3,2},{4,5},{5,4},{6,7},{7,6},{8,9},{9,8},{10,11... | collective-permute-start | bytes 2359304 | tf_op jit(solution)/shard_map/ppermute | solution.py:490
  277.5 17.6 %collective-permute-start.41 = (bf16[4,32,1024]{2,1,0:T(8,128)(2,1)}, bf16[4,32,1024]{2,1,0:T(8,128)(2,1)}, u32[]{:S(2)}, u32[]{:S(2)}) collective-permute-start(bf16[4,32,1024]{2,1,0:T(8,128)(2,1)} %get-tuple-element.76), channel_id=1, source_target_pairs={{0,8},{1,9},{2,10},{3,11},{4,12},{5,13},{6,14},{7,15},{8,0},{9,1},... | collective-permute-start | bytes 786440 | tf_op jit(solution)/shard_map/ppermute | solution.py:490
  284.8 17.0 %collective-permute-start.42 = (bf16[4,32,1024]{2,1,0:T(8,128)(2,1)S(1)}, bf16[4,32,1024]{2,1,0:T(8,128)(2,1)}, u32[]{:S(2)}, u32[]{:S(2)}) collective-permute-start(bf16[4,32,1024]{2,1,0:T(8,128)(2,1)S(1)} %get-tuple-element.77), channel_id=1, source_target_pairs={{0,12},{1,13},{2,14},{3,15},{4,8},{5,9},{6,10},{7,11},{8,4},{9,5},... | collective-permute-start | bytes 786440 | tf_op jit(solution)/shard_map/ppermute | solution.py:490
  305.5 25.0 %collective-permute-start.34 = (bf16[2,96,1024]{2,1,0:T(8,128)(2,1)}, bf16[2,96,1024]{2,1,0:T(8,128)(2,1)}, u32[]{:S(2)}, u32[]{:S(2)}) collective-permute-start(bf16[2,96,1024]{2,1,0:T(8,128)(2,1)} %slice.127), channel_id=1, source_target_pairs={{0,1},{1,0},{2,3},{3,2},{4,5},{5,4},{6,7},{7,6},{8,9},{9,8},{10,11... | collective-permute-start | bytes 1179656 | tf_op jit(solution)/shard_map/ppermute | solution.py:490
  306.5 59.7 %collective-permute-start.43 = (bf16[32,1024]{1,0:T(8,128)(2,1)}, bf16[32,1024]{1,0:T(8,128)(2,1)}, u32[]{:S(2)}, u32[]{:S(2)}) collective-permute-start(bf16[32,1024]{1,0:T(8,128)(2,1)} %get-tuple-element.102), channel_id=1, source_target_pairs={{0,1},{1,0},{2,3},{3,2},{4,5},{5,4},{6,7},{7,6},{8,9},{9,8},{10,11... | collective-permute-start | bytes 196616 | tf_op jit(solution)/shard_map/ppermute | solution.py:490
  307.6 61.4 %collective-permute-start.44 = (bf16[32,1024]{1,0:T(8,128)(2,1)}, bf16[32,1024]{1,0:T(8,128)(2,1)}, u32[]{:S(2)}, u32[]{:S(2)}) collective-permute-start(bf16[32,1024]{1,0:T(8,128)(2,1)} %get-tuple-element.104), channel_id=1, source_target_pairs={{0,2},{1,3},{2,0},{3,1},{4,6},{5,7},{6,4},{7,5},{8,10},{9,11},{10,... | collective-permute-start | bytes 196616 | tf_op jit(solution)/shard_map/ppermute | solution.py:490
  307.9 61.1 %collective-permute-start.45 = (bf16[32,1024]{1,0:T(8,128)(2,1)}, bf16[32,1024]{1,0:T(8,128)(2,1)}, u32[]{:S(2)}, u32[]{:S(2)}) collective-permute-start(bf16[32,1024]{1,0:T(8,128)(2,1)} %get-tuple-element.103), channel_id=1, source_target_pairs={{0,3},{1,2},{2,1},{3,0},{4,7},{5,6},{6,5},{7,4},{8,11},{9,10},{10,... | collective-permute-start | bytes 196616 | tf_op jit(solution)/shard_map/ppermute | solution.py:490
  311.5 22.4 %collective-permute-start.37 = (bf16[2,96,1024]{2,1,0:T(8,128)(2,1)}, bf16[2,96,1024]{2,1,0:T(8,128)(2,1)}, u32[]{:S(2)}, u32[]{:S(2)}) collective-permute-start(bf16[2,96,1024]{2,1,0:T(8,128)(2,1)} %slice.131), channel_id=1, source_target_pairs={{0,2},{1,3},{2,0},{3,1},{4,6},{5,7},{6,4},{7,5},{8,10},{9,11},{10,... | collective-permute-start | bytes 1179656 | tf_op jit(solution)/shard_map/ppermute | solution.py:490
  325.5 12.3 %all-to-all-start.3 = ((f32[16,2,3,8,128]{4,3,2,1,0:T(8,128)}), f32[16,2,3,8,128]{4,3,2,1,0:T(8,128)S(1)}, u32[]{:S(2)}, u32[]{:S(2)}) async-start(f32[16,2,3,8,128]{4,3,2,1,0:T(8,128)} %get-tuple-element.56), calls=%async_computation.3 | async-start | bytes 786432 | tf_op jit(solution)/shard_map/all_to_all | solution.py:551
  332.7 38.6 %collective-permute-start.35 = (bf16[96,1024]{1,0:T(8,128)(2,1)}, bf16[96,1024]{1,0:T(8,128)(2,1)}, u32[]{:S(2)}, u32[]{:S(2)}) collective-permute-start(bf16[96,1024]{1,0:T(8,128)(2,1)} %slice_bitcast_fusion.2), channel_id=1, source_target_pairs={{0,4},{1,5},{2,6},{3,7},{4,0},{5,1},{6,2},{7,3},{8,12},{9,13},{10,... | collective-permute-start | bytes 589832 | tf_op jit(solution)/shard_map/ppermute | solution.py:490
  352.8 75.2 %collective-permute-start.18 = (f32[768,1024]{1,0:T(8,128)}, f32[768,1024]{1,0:T(8,128)}, u32[]{:S(2)}, u32[]{:S(2)}) collective-permute-start(f32[768,1024]{1,0:T(8,128)} %get-tuple-element.59), channel_id=1, source_target_pairs={{0,16},{16,0},{1,17},{17,1},{2,18},{18,2},{3,19},{19,3},{4,20},{20... | collective-permute-start | bytes 9437192 | tf_op jit(solution)/shard_map/ppermute | solution.py:494
  366.3 14.8 %collective-permute-start.38 = (bf16[96,1024]{1,0:T(8,128)(2,1)S(1)}, bf16[96,1024]{1,0:T(8,128)(2,1)S(1)}, u32[]{:S(2)}, u32[]{:S(2)}) collective-permute-start(bf16[96,1024]{1,0:T(8,128)(2,1)S(1)} %get-tuple-element.98), channel_id=1, source_target_pairs={{0,8},{1,9},{2,10},{3,11},{4,12},{5,13},{6,14},{7,15},{8,0},{9,1},... | collective-permute-start | bytes 589832 | tf_op jit(solution)/shard_map/ppermute | solution.py:490
  369.0 17.0 %collective-permute-start.39 = (bf16[96,1024]{1,0:T(8,128)(2,1)S(1)}, bf16[96,1024]{1,0:T(8,128)(2,1)S(1)}, u32[]{:S(2)}, u32[]{:S(2)}) collective-permute-start(bf16[96,1024]{1,0:T(8,128)(2,1)S(1)} %get-tuple-element.99), channel_id=1, source_target_pairs={{0,12},{1,13},{2,14},{3,15},{4,8},{5,9},{6,10},{7,11},{8,4},{9,5},... | collective-permute-start | bytes 589832 | tf_op jit(solution)/shard_map/ppermute | solution.py:490
  369.1 19.3 %collective-permute-start.27 = (bf16[4,32,1024]{2,1,0:T(8,128)(2,1)S(1)}, bf16[4,32,1024]{2,1,0:T(8,128)(2,1)S(1)}, u32[]{:S(2)}, u32[]{:S(2)}) collective-permute-start(bf16[4,32,1024]{2,1,0:T(8,128)(2,1)S(1)} %get-tuple-element.66), channel_id=1, source_target_pairs={{0,4},{1,5},{2,6},{3,7},{4,0},{5,1},{6,2},{7,3},{8,12},{9,13},{10,... | collective-permute-start | bytes 786440 | tf_op jit(solution)/shard_map/ppermute | solution.py:490
  371.3 42.9 %collective-permute-start.20 = (bf16[4,96,1024]{2,1,0:T(8,128)(2,1)}, bf16[4,96,1024]{2,1,0:T(8,128)(2,1)}, u32[]{:S(2)}, u32[]{:S(2)}) collective-permute-start(bf16[4,96,1024]{2,1,0:T(8,128)(2,1)} %get-tuple-element.62), channel_id=1, source_target_pairs={{0,2},{1,3},{2,0},{3,1},{4,6},{5,7},{6,4},{7,5},{8,10},{9,11},{10,... | collective-permute-start | bytes 2359304 | tf_op jit(solution)/shard_map/ppermute | solution.py:490
  387.1 29.0 %collective-permute-start.23 = (bf16[4,96,1024]{2,1,0:T(8,128)(2,1)}, bf16[4,96,1024]{2,1,0:T(8,128)(2,1)}, u32[]{:S(2)}, u32[]{:S(2)}) collective-permute-start(bf16[4,96,1024]{2,1,0:T(8,128)(2,1)} %get-tuple-element.64), channel_id=1, source_target_pairs={{0,1},{1,0},{2,3},{3,2},{4,5},{5,4},{6,7},{7,6},{8,9},{9,8},{10,11... | collective-permute-start | bytes 2359304 | tf_op jit(solution)/shard_map/ppermute | solution.py:490
  388.3 16.2 %collective-permute-start.28 = (bf16[4,32,1024]{2,1,0:T(8,128)(2,1)S(1)}, bf16[4,32,1024]{2,1,0:T(8,128)(2,1)}, u32[]{:S(2)}, u32[]{:S(2)}) collective-permute-start(bf16[4,32,1024]{2,1,0:T(8,128)(2,1)S(1)} %get-tuple-element.67), channel_id=1, source_target_pairs={{0,8},{1,9},{2,10},{3,11},{4,12},{5,13},{6,14},{7,15},{8,0},{9,1},... | collective-permute-start | bytes 786440 | tf_op jit(solution)/shard_map/ppermute | solution.py:490
  388.3 24.6 %collective-permute-start.29 = (bf16[4,32,1024]{2,1,0:T(8,128)(2,1)S(1)}, bf16[4,32,1024]{2,1,0:T(8,128)(2,1)}, u32[]{:S(2)}, u32[]{:S(2)}) collective-permute-start(bf16[4,32,1024]{2,1,0:T(8,128)(2,1)S(1)} %get-tuple-element.68), channel_id=1, source_target_pairs={{0,12},{1,13},{2,14},{3,15},{4,8},{5,9},{6,10},{7,11},{8,4},{9,5},... | collective-permute-start | bytes 786440 | tf_op jit(solution)/shard_map/ppermute | solution.py:490
  404.5 53.8 %collective-permute-start.16 = (bf16[768,1024]{1,0:T(8,128)(2,1)}, bf16[768,1024]{1,0:T(8,128)(2,1)S(1)}, u32[]{:S(2)}, u32[]{:S(2)}) collective-permute-start(bf16[768,1024]{1,0:T(8,128)(2,1)} %get-tuple-element.47), channel_id=1, source_target_pairs={{0,16},{16,0},{1,17},{17,1},{2,18},{18,2},{3,19},{19,3},{4,20},{20... | collective-permute-start | bytes 4718600 | tf_op jit(solution)/shard_map/ppermute | solution.py:494
  415.7 9.5 %collective-permute-start.21 = (bf16[2,96,1024]{2,1,0:T(8,128)(2,1)S(1)}, bf16[2,96,1024]{2,1,0:T(8,128)(2,1)S(1)}, u32[]{:S(2)}, u32[]{:S(2)}) collective-permute-start(bf16[2,96,1024]{2,1,0:T(8,128)(2,1)S(1)} %slice.115), channel_id=1, source_target_pairs={{0,1},{1,0},{2,3},{3,2},{4,5},{5,4},{6,7},{7,6},{8,9},{9,8},{10,11... | collective-permute-start | bytes 1179656 | tf_op jit(solution)/shard_map/ppermute | solution.py:490
  417.7 9.2 %collective-permute-start.24 = (bf16[2,96,1024]{2,1,0:T(8,128)(2,1)S(1)}, bf16[2,96,1024]{2,1,0:T(8,128)(2,1)S(1)}, u32[]{:S(2)}, u32[]{:S(2)}) collective-permute-start(bf16[2,96,1024]{2,1,0:T(8,128)(2,1)S(1)} %slice.119), channel_id=1, source_target_pairs={{0,2},{1,3},{2,0},{3,1},{4,6},{5,7},{6,4},{7,5},{8,10},{9,11},{10,... | collective-permute-start | bytes 1179656 | tf_op jit(solution)/shard_map/ppermute | solution.py:490
  417.8 17.8 %collective-permute-start.30 = (bf16[32,1024]{1,0:T(8,128)(2,1)S(1)}, bf16[32,1024]{1,0:T(8,128)(2,1)S(1)}, u32[]{:S(2)}, u32[]{:S(2)}) collective-permute-start(bf16[32,1024]{1,0:T(8,128)(2,1)S(1)} %get-tuple-element.105), channel_id=1, source_target_pairs={{0,1},{1,0},{2,3},{3,2},{4,5},{5,4},{6,7},{7,6},{8,9},{9,8},{10,11... | collective-permute-start | bytes 196616 | tf_op jit(solution)/shard_map/ppermute | solution.py:490
  425.3 10.5 %collective-permute-start.31 = (bf16[32,1024]{1,0:T(8,128)(2,1)S(1)}, bf16[32,1024]{1,0:T(8,128)(2,1)S(1)}, u32[]{:S(2)}, u32[]{:S(2)}) collective-permute-start(bf16[32,1024]{1,0:T(8,128)(2,1)S(1)} %get-tuple-element.107), channel_id=1, source_target_pairs={{0,2},{1,3},{2,0},{3,1},{4,6},{5,7},{6,4},{7,5},{8,10},{9,11},{10,... | collective-permute-start | bytes 196616 | tf_op jit(solution)/shard_map/ppermute | solution.py:490
  427.0 10.3 %collective-permute-start.32 = (bf16[32,1024]{1,0:T(8,128)(2,1)S(1)}, bf16[32,1024]{1,0:T(8,128)(2,1)S(1)}, u32[]{:S(2)}, u32[]{:S(2)}) collective-permute-start(bf16[32,1024]{1,0:T(8,128)(2,1)S(1)} %get-tuple-element.106), channel_id=1, source_target_pairs={{0,3},{1,2},{2,1},{3,0},{4,7},{5,6},{6,5},{7,4},{8,11},{9,10},{10,... | collective-permute-start | bytes 196616 | tf_op jit(solution)/shard_map/ppermute | solution.py:490
  432.2 45.7 %collective-permute-start.19 = (bf16[768,1024]{1,0:T(8,128)(2,1)}, bf16[768,1024]{1,0:T(8,128)(2,1)}, u32[]{:S(2)}, u32[]{:S(2)}) collective-permute-start(bf16[768,1024]{1,0:T(8,128)(2,1)} %get-tuple-element.90), channel_id=1, source_target_pairs={{0,16},{16,0},{1,17},{17,1},{2,18},{18,2},{3,19},{19,3},{4,20},{20... | collective-permute-start | bytes 4718600 | tf_op jit(solution)/shard_map/ppermute | solution.py:494
  435.7 10.8 %collective-permute-start.25 = (bf16[96,1024]{1,0:T(8,128)(2,1)S(1)}, bf16[96,1024]{1,0:T(8,128)(2,1)S(1)}, u32[]{:S(2)}, u32[]{:S(2)}) collective-permute-start(bf16[96,1024]{1,0:T(8,128)(2,1)S(1)} %get-tuple-element.100), channel_id=1, source_target_pairs={{0,8},{1,9},{2,10},{3,11},{4,12},{5,13},{6,14},{7,15},{8,0},{9,1},... | collective-permute-start | bytes 589832 | tf_op jit(solution)/shard_map/ppermute | solution.py:490
  437.2 18.6 %collective-permute-start.26 = (bf16[96,1024]{1,0:T(8,128)(2,1)S(1)}, bf16[96,1024]{1,0:T(8,128)(2,1)S(1)}, u32[]{:S(2)}, u32[]{:S(2)}) collective-permute-start(bf16[96,1024]{1,0:T(8,128)(2,1)S(1)} %get-tuple-element.101), channel_id=1, source_target_pairs={{0,12},{1,13},{2,14},{3,15},{4,8},{5,9},{6,10},{7,11},{8,4},{9,5},... | collective-permute-start | bytes 589832 | tf_op jit(solution)/shard_map/ppermute | solution.py:490
  443.4 26.6 %collective-permute-start.47 = (f32[3,1000]{1,0:T(4,128)}, f32[3,1000]{1,0:T(4,128)}, u32[]{:S(2)}, u32[]{:S(2)}) collective-permute-start(f32[3,1000]{1,0:T(4,128)} %bitcast.106), channel_id=1, source_target_pairs={{0,16},{16,0},{1,17},{17,1},{2,18},{18,2},{3,19},{19,3},{4,20},{20... | collective-permute-start | bytes 36008 | tf_op jit(solution)/shard_map/ppermute | solution.py:494
  457.2 14.2 %collective-permute-start.46 = (f32[128,1024]{1,0:T(8,128)}, f32[128,1024]{1,0:T(8,128)}, u32[]{:S(2)}, u32[]{:S(2)}) collective-permute-start(f32[128,1024]{1,0:T(8,128)} %get-tuple-element.94), channel_id=1, source_target_pairs={{0,16},{16,0},{1,17},{17,1},{2,18},{18,2},{3,19},{19,3},{4,20},{20... | collective-permute-start | bytes 1572872 | tf_op jit(solution)/shard_map/ppermute | solution.py:494
  (40 other events, 937.3 us)

commit v2 on v1

--- a/solution.py
+++ b/solution.py
@@ -13,7 +13,6 @@
 HALF = SUB * LANES
 COLUMNS = 256
 UPPER = 96
-VMEM_BYTES = 52 << 20
 F32 = jnp.float32
 BF16 = jnp.bfloat16
 VMEM = pl.BlockSpec(memory_space=pltpu.VMEM)
@@ -25,54 +24,137 @@
     return jax.ShapeDtypeStruct(shape, dtype)
 
 
-def params(**more):
-    return pltpu.CompilerParams(vmem_limit_bytes=VMEM_BYTES, **more)
-
-
-def spread_kernel(width, in_ref, out_ref):
+def params(mebibytes):
+    return pltpu.CompilerParams(vmem_limit_bytes=mebibytes << 20)
+
+
+def turned(x, shift, stride):
+    if shift % LANES:
+        x = pltpu.roll(x, shift % LANES, 1)
+    return pltpu.roll(x, 0, 1, stride=stride, stride_axis=0)
+
+
+def cut_kernel(width, in_ref, out_ref, lines, pieces):
     total = in_ref.shape[1]
-    lane = lax.broadcasted_iota(jnp.int32, (in_ref.shape[0], LANES), 1)
-
-    def aligned(q):
-        low, high = q * LANES, min((q + 1) * LANES, total)
-        if high - low == LANES:
-            return in_ref[:, low:high].astype(F32)
-        tail = jnp.zeros((in_ref.shape[0], LANES - (high - low)), F32)
-        return jnp.concatenate([in_ref[:, low:high].astype(F32), tail], axis=1)
-
+    full, rest = divmod(total, HALF)
+    for g in range(full):
+        lines[SUB * (g + 1) : SUB * (g + 2), :] = in_ref[:, HALF * g : HALF * (g + 1)].reshape(SUB, LANES)
+    for k in range(pl.cdiv(rest, LANES)):
+        at = HALF * full + LANES * k
+        size = min(LANES, total - at)
+        row = SUB * (full + 1) + k
+        lines[row : row + 1, :size] = in_ref[:, at : at + size]
+    count = total // width
+    gap = LANES - width
+    lane = lax.broadcasted_iota(jnp.int32, (SUB, LANES), 1)
+    line = lax.broadcasted_iota(jnp.int32, (SUB, LANES), 0)
+    for i in range(0, count, SUB):
+        first, offset = divmod(width * i, LANES)
+        at = offset - gap * line + lane
+
+        def taken(k):
+            start = SUB + first + k
+            return turned(lines[start : start + SUB, :], -offset, gap)
+
+        value = taken(0)
+        if offset < SUB * gap:
+            value = jnp.where(at < 0, taken(-1), value)
+        value = jnp.where(at >= LANES, taken(1), value)
+        pieces[i : i + SUB, :] = jnp.where(lane < width, value, 0.0)
+    valid = lax.broadcasted_iota(jnp.int32, (LANES, LANES), 0) < count // (2 * SUB)
     for j in range(2 * SUB):
-        q, shift = divmod(width * j, LANES)
-        piece = aligned(q)
-        if shift:
-            piece = pltpu.roll(piece, LANES - shift, 1)
-            if width > LANES - shift:
-                after = pltpu.roll(aligned(q + 1), LANES - shift, 1)
-                piece = jnp.where(lane < LANES - shift, piece, after)
-        piece = jnp.where(lane < width, piece, 0.0).astype(out_ref.dtype)
-        out_ref[j // SUB, :, (j % SUB) * LANES : (j % SUB + 1) * LANES] = piece
-
-
-def spread(natural, width, rows):
-    count, total = natural.shape
+        block = pieces[pl.ds(j, LANES, stride=2 * SUB), :]
+        block = jnp.where(valid, block, 0.0).astype(BF16)
+        out_ref[j // SUB, :, (j % SUB) * LANES : (j % SUB + 1) * LANES] = block
+
+
+def cut(flat, width):
+    total = flat.shape[1]
+    return pl.pallas_call(
+        partial(cut_kernel, width),
+        in_specs=[VMEM],
+        out_specs=VMEM,
+        out_shape=shaped((2, LANES, HALF), BF16),
+        scratch_shapes=[
+            pltpu.VMEM(((total // HALF + 3) * SUB, LANES), F32),
+            pltpu.VMEM((2 * HALF, LANES), F32),
+        ],
+        compiler_params=params(8),
+        name="cut",
+    )(flat)
+
+
+def spread_kernel(width, scal, in_ref, *rest):
+    out_refs, lines = rest[:-1], rest[-1]
+    total = in_ref.shape[1]
+    lines[0:total, :] = in_ref[0].astype(F32)
+    frames = in_ref.shape[2]
+    lane = lax.broadcasted_iota(jnp.int32, (frames, LANES), 1)
+    for out_ref, half in zip(out_refs, (scal[1], 1 - scal[1])):
+        for j in range(SUB):
+            below, shift = divmod(width * j, SUB)
+            start = pl.multiple_of(half * (SUB * width) + below * SUB, SUB)
+            block = lines[pl.ds(start, LANES + SUB), :][shift : shift + LANES]
+            block = jnp.where(lane < width, block.T, 0.0).astype(BF16)
+            out_ref[:, j * LANES : (j + 1) * LANES] = block
+
+
+def spread(scal, turned_over, halves):
+    count, total, frames = turned_over.shape
+    width = total // (2 * SUB)
     return pl.pallas_call(
         partial(spread_kernel, width),
-        grid=(count // rows,),
-        in_specs=[pl.BlockSpec((rows, total), lambda i: (i, 0))],
-        out_specs=pl.BlockSpec((2, rows, HALF), lambda i: (0, i, 0)),
-        out_shape=shaped((2, count, HALF), BF16),
-        compiler_params=params(),
+        grid=(count,),
+        in_specs=[SMEM, pl.BlockSpec((1, total, frames), lambda i: (i, 0, 0))],
+        out_specs=[pl.BlockSpec((frames, HALF), lambda i: (i, 0))] * halves,
+        out_shape=[shaped((count * frames, HALF), BF16)] * halves,
+        scratch_shapes=[pltpu.VMEM((total + SUB, frames), F32)],
+        compiler_params=params(8),
         name="spread",
-    )(natural)
-
-
-def join_kernel(width, scal, own_ref, other_ref, out_ref):
+    )(scal, turned_over)
+
+
+def join_kernel(width, scal, *rest):
+    in_refs, (out_ref, lines) = rest[:-2], rest[-2:]
+
+    def write(halves):
+        for j in range(2 * SUB):
+            at = (j % SUB) * LANES
+            block = halves[j // SUB][:, at : at + LANES].astype(F32).T
+            lines[width * j : width * (j + 1), :] = block[:width]
+        out_ref[0] = lines[...].astype(out_ref.dtype)
+
+    for core in (0, 1):
+
+        @pl.when(scal[1] == core)
+        def _(core=core):
+            write(in_refs[2 * core : 2 * core + 2])
+
+
+def join(scal, halves, total, frames):
+    width = total // (2 * SUB)
+    count = halves[0].shape[0] // frames
+    half = pl.BlockSpec((frames, HALF), lambda i: (i, 0))
+    return pl.pallas_call(
+        partial(join_kernel, width),
+        grid=(count,),
+        in_specs=[SMEM] + [half] * 4,
+        out_specs=pl.BlockSpec((1, total, frames), lambda i: (i, 0, 0)),
+        out_shape=shaped((count, total, frames), halves[0].dtype),
+        scratch_shapes=[pltpu.VMEM((total, frames), F32)],
+        compiler_params=params(8),
+        name="join",
+    )(scal, *halves)
+
+
+def rows_kernel(width, scal, own_ref, other_ref, out_ref):
     total = out_ref.shape[1]
     lane = lax.broadcasted_iota(jnp.int32, (out_ref.shape[0], LANES), 1)
 
     def write(halves):
         def block(j):
             at = (j % SUB) * LANES
-            return halves[j // SUB][:, at : at + LANES].astype(F32)
+            return halves[j // SUB][:, at : at + LANES]
 
         for q in range(pl.cdiv(total, LANES)):
             j, shift = divmod(LANES * q, width)
@@ -83,7 +165,7 @@
                 after = pltpu.roll(block(j + 1), width - shift, 1)
                 piece = jnp.where(lane < width - shift, piece, after)
             keep = min(LANES, total - q * LANES)
-            out_ref[:, q * LANES : q * LANES + keep] = piece[:, :keep].astype(out_ref.dtype)
+            out_ref[:, q * LANES : q * LANES + keep] = piece[:, :keep]
 
     @pl.when(scal[1] == 0)
     def _():
@@ -94,25 +176,44 @@
         write((other_ref, own_ref))
 
 
-def join(scal, own, other, total, rows):
+def natural_rows(scal, own, other, total):
     width = total // (2 * SUB)
     count = own.shape[0]
-    half = pl.BlockSpec((rows, HALF), lambda i: (i, 0))
-    return pl.pallas_call(
-        partial(join_kernel, width),
-        grid=(count // rows,),
+    half = pl.BlockSpec((LANES, HALF), lambda i: (i, 0))
+    return pl.pallas_call(
+        partial(rows_kernel, width),
+        grid=(count // LANES,),
         in_specs=[SMEM, half, half],
-        out_specs=pl.BlockSpec((rows, total), lambda i: (i, 0)),
-        out_shape=shaped((count, total), own.dtype),
-        compiler_params=params(),
-        name="join",
+        out_specs=pl.BlockSpec((LANES, total), lambda i: (i, 0)),
+        out_shape=shaped((count, total)),
+        compiler_params=params(8),
+        name="natural_rows",
     )(scal, own, other)
 
 
-def load_weight(plan, layer, scal, piece_refs, weight, sems):
+def finish_kernel(scal, g_ref, mine_ref, theirs_ref, out_ref, sent_ref):
+    grad = (g_ref[...].astype(F32) + (mine_ref[...] + theirs_ref[...])).astype(BF16)
+    out_ref[...] = grad
+    sent_ref[...] = jnp.where(scal[1] == 0, g_ref[...], grad)
+
+
+def finish(scal, g, mine, theirs, frames):
+    block = pl.BlockSpec((frames, HALF), lambda i: (i, 0))
+    return pl.pallas_call(
+        finish_kernel,
+        grid=(g.shape[0] // frames,),
+        in_specs=[SMEM] + [block] * 3,
+        out_specs=[block] * 2,
+        out_shape=[shaped(g.shape, BF16)] * 2,
+        compiler_params=params(8),
+        name="finish",
+    )(scal, g, mine, theirs)
+
+
+def load_weight(plan, scal, piece_refs, weight, sems):
     copies = []
     for i, (ref_index, lead, mask, row, rows) in enumerate(plan):
-        source = piece_refs[ref_index].at[(*lead, layer)]
+        source = piece_refs[ref_index].at[lead] if lead else piece_refs[ref_index]
         if mask is None:
             target = weight.at[pl.ds(row, rows), :]
         else:
@@ -129,10 +230,10 @@
     return frame < length
 
 
-def project_kernel(plan, layer, sizes, scal, own_ref, other_ref, *rest):
+def project_kernel(plan, sizes, scal, own_ref, other_ref, *rest):
     micro, views, frames = sizes
     piece_refs, (z_ref, stats_ref, weight, sems) = rest[:-4], rest[-4:]
-    for copy in load_weight(plan, layer, scal, piece_refs, weight, sems):
+    for copy in load_weight(plan, scal, piece_refs, weight, sems):
         copy.wait()
     sequences = micro * views
     own_at = pl.multiple_of(scal[1] * HALF, HALF)
@@ -166,11 +267,11 @@
                     stats_ref[i, m, 1, j : j + 1, :] = second[:, k * LANES : (k + 1) * LANES]
 
 
-def project(plan, layer, sizes, copies, scal, own, other, pieces):
+def project(plan, sizes, copies, scal, own, other, pieces):
     micro, views, frames = sizes
     rows = own.shape[0]
     return pl.pallas_call(
-        partial(project_kernel, plan, layer, sizes),
+        partial(project_kernel, plan, sizes),
         in_specs=[SMEM, VMEM, VMEM] + [ANY] * len(pieces),
         out_specs=[VMEM, VMEM],
         out_shape=[shaped((rows * SUB, LANES)), shaped((copies, micro, 2, SUB, LANES))],
@@ -178,7 +279,7 @@
             pltpu.VMEM((2 * HALF, HALF), BF16),
             pltpu.SemaphoreType.DMA((len(plan),)),
         ],
-        compiler_params=params(),
+        compiler_params=params(20),
         cost_estimate=pl.CostEstimate(
             flops=4 * rows * HALF * HALF, bytes_accessed=12 * HALF * HALF, transcendentals=0
         ),
@@ -258,7 +359,7 @@
             shaped(((frames + 1) * step, LANES)),
             shaped((micro, 2, SUB, LANES)),
         ],
-        compiler_params=params(),
+        compiler_params=params(14),
         cost_estimate=pl.CostEstimate(
             flops=8 * z.size, bytes_accessed=12 * z.size, transcendentals=z.size
         ),
@@ -348,7 +449,7 @@
             pltpu.VMEM(z.shape, F32),
             pltpu.VMEM(z.shape, F32),
         ],
-        compiler_params=params(),
+        compiler_params=params(26),
         cost_estimate=pl.CostEstimate(
             flops=20 * z.size, bytes_accessed=14 * z.size, transcendentals=z.size
         ),
@@ -385,7 +486,7 @@
             shaped((copies, micro, 3, SUB, LANES)),
         ],
         scratch_shapes=[pltpu.VMEM(z.shape, F32)],
-        compiler_params=params(),
+        compiler_params=params(28),
         cost_estimate=pl.CostEstimate(
             flops=20 * z.size, bytes_accessed=24 * z.size, transcendentals=z.size
         ),
@@ -393,10 +494,10 @@
     )(scal, par, norm, z, h, base, mine, theirs)
 
 
-def unproject_kernel(plan, layer, sizes, scal, totals, sums_ref, par_ref, norm_ref, z_ref, p_ref, *rest):
+def unproject_kernel(plan, sizes, scal, totals, sums_ref, par_ref, norm_ref, z_ref, p_ref, *rest):
     micro, views, frames = sizes
     piece_refs, (dz_ref, mine_ref, theirs_ref, weight, sems) = rest[:-5], rest[-5:]
-    copies = load_weight(plan, layer, scal, piece_refs, weight, sems)
+    copies = load_weight(plan, scal, piece_refs, weight, sems)
     step = micro * views * SUB
     for m in range(micro):
         first = jnp.sum(sums_ref[:, m, 0], axis=0) / totals[m]
@@ -425,10 +526,10 @@
             )
 
 
-def unproject(plan, layer, sizes, scal, totals, sums, par, norm, z, p, pieces):
+def unproject(plan, sizes, scal, totals, sums, par, norm, z, p, pieces):
     rows = z.shape[0] // SUB
     return pl.pallas_call(
-        partial(unproject_kernel, plan, layer, sizes),
+        partial(unproject_kernel, plan, sizes),
         in_specs=[SMEM, SMEM] + [VMEM] * 5 + [ANY] * len(pieces),
         out_specs=[VMEM] * 3,
         out_shape=[shaped((rows, HALF), BF16), shaped((rows, HALF)), shaped((rows, HALF))],
@@ -436,7 +537,7 @@
             pltpu.VMEM((2 * HALF, HALF), BF16),
             pltpu.SemaphoreType.DMA((len(plan),)),
         ],
-        compiler_params=params(),
+        compiler_params=params(26),
         cost_estimate=pl.CostEstimate(
             flops=4 * rows * HALF * HALF, bytes_accessed=24 * HALF * HALF, transcendentals=0
         ),
@@ -460,7 +561,8 @@
         else:
             start = pl.multiple_of((scal[0] ^ mask) * LANES + row, 16)
             source = grad.at[pl.ds(start, count), :]
-        copy = pltpu.make_async_copy(source, out_refs[ref_index].at[lead], sems.at[i])
+        target = out_refs[ref_index].at[lead] if lead else out_refs[ref_index]
+        copy = pltpu.make_async_copy(source, target, sems.at[i])
         copy.start()
         copies.append(copy)
     for copy in copies:
@@ -477,7 +579,7 @@
             pltpu.VMEM((2 * HALF, HALF), dtype),
             pltpu.SemaphoreType.DMA((len(plan),)),
         ],
-        compiler_params=params(),
+        compiler_params=params(20),
         cost_estimate=pl.CostEstimate(
             flops=4 * own.shape[0] * HALF * HALF, bytes_accessed=12 * HALF * HALF, transcendentals=0
         ),
@@ -497,28 +599,24 @@
 ROUTED = 16
 FIRST = (0, 4, 1, 5, 2, 6, 3, 7)
 SECOND = (8, 12, 10, 14, 9, 13, 11, 15)
-
-
-def gather_pieces(shard):
-    upper, lower = shard[:, :UPPER], shard[:, UPPER:]
-    third = [lower] + [flip(lower, m) for m in (1, 2, 3)]
-    along = [upper] + [flip(upper, m) for m in (4, 8, 12)]
-    third = jnp.stack(third)
+WHOLE = [(0, (), None, 0, 2 * HALF)]
+together = lax.optimization_barrier
+
+
+def gather_pieces(shard, later):
+    upper, lower = shard[:UPPER], shard[UPPER:]
+    got = [flip(upper, m) for m in (4, 8, 12)] + [flip(lower, m) for m in (1, 2, 3)]
+    *got, later = together((*got, later))
+    a0, b0 = jnp.stack([upper, got[0]]), jnp.stack(got[1:3])
+    third = jnp.stack([lower, *got[3:]])
+    a1, b1 = flip(a0, 1), flip(b0, 2)
     lows = [third] + [flip(third, m) for m in (4, 8, 12)]
-    a0, b0 = jnp.stack(along[:2]), jnp.stack(along[2:])
-    a1, b1 = flip(a0, 1), flip(b0, 2)
     a01, b01 = jnp.concatenate([a0, a1]), jnp.concatenate([b0, b1])
     a2, b2 = flip(a01, 2), flip(b01, 1)
-    pieces = [a01, a2, b01, b2] + lows
-    plan = []
-    for ref, masks in ((0, FIRST[:4]), (1, FIRST[4:]), (2, SECOND[:4]), (3, SECOND[4:])):
-        plan += [(ref, (i,), m, 0, UPPER) for i, m in enumerate(masks)]
-    for k in range(4):
-        plan += [(4 + k, (i,), 4 * k + i, UPPER, LANES - UPPER) for i in range(4)]
-    return pieces, plan
-
-
-def scatter_plan():
+    return [a01, a2, b01, b2] + lows, later
+
+
+def routed_plan():
     plan, shapes = [], []
     for k, masks in enumerate((FIRST[:4], FIRST[4:], SECOND[:4], SECOND[4:])):
         plan += [(k, (i,), m, 0, UPPER) for i, m in enumerate(masks)]
@@ -533,16 +631,20 @@
     return sum(t.astype(F32) for t in terms)
 
 
-def scatter_pieces(parts):
+def scatter_pieces(parts, beside_first, beside_second):
     a01, a2, b01, b2, *lows = parts
-    low = add(lows[0], *[flip(lows[k], 4 * k) for k in (1, 2, 3)]).astype(BF16)
-    a01 = add(a01, flip(a2, 2)).astype(BF16)
-    b01 = add(b01, flip(b2, 1)).astype(BF16)
-    a0 = add(a01[:2], flip(a01[2:], 1)).astype(BF16)
-    b0 = add(b01[:2], flip(b01[2:], 2)).astype(BF16)
-    lower = add(low[0], *[flip(low[m], m) for m in (1, 2, 3)])
+    got = [flip(lows[k], 4 * k) for k in (1, 2, 3)] + [flip(a2, 2), flip(b2, 1)]
+    *got, beside_first = together((*got, beside_first))
+    low = add(lows[0], *got[:3]).astype(BF16)
+    a01 = add(a01, got[3]).astype(BF16)
+    b01 = add(b01, got[4]).astype(BF16)
+    got = [flip(a01[2:], 1), flip(b01[2:], 2)] + [flip(low[m], m) for m in (1, 2, 3)]
+    *got, beside_second = together((*got, beside_second))
+    a0 = add(a01[:2], got[0]).astype(BF16)
+    b0 = add(b01[:2], got[1]).astype(BF16)
+    lower = add(low[0], *got[2:])
     upper = add(a0[0], flip(a0[1], 4), flip(b0[0], 8), flip(b0[1], 12))
-    return jnp.concatenate([upper, lower])
+    return jnp.concatenate([upper, lower]), beside_first, beside_second
 
 
 def exchange(x):
@@ -584,58 +686,60 @@
     par = both(vectors, True)
 
     if routed:
-        shard = jnp.pad(weights.reshape(width, total), ((0, LANES - width), (0, 0)))
-        shard = jnp.stack(both(spread(shard, width, LANES), True))
-        pieces, plan = gather_pieces(shard)
+        shards = both(cut(weights, width), True)
+        pieces0, later = gather_pieces(*shards)
+        pieces1 = [lax.all_gather(later, "dp").reshape(2 * HALF, HALF)]
+        plan, shapes = routed_plan()
     else:
         whole = lax.all_gather(weights[0].astype(BF16), "dp", axis=0, tiled=True)
-        whole = jnp.stack(both(blocks_of(whole.reshape(total, total), width), True))
-        pieces, plan = [whole], [(0, (), None, 0, 2 * HALF)]
-
-    def halves_of(x):
-        spreaded = spread(x.reshape(rows, total), width, frames)
-        return [lax.dynamic_index_in_dim(spreaded, k, 0, keepdims=False) for k in (section, 1 - section)]
-
-    x_own, x_other = halves_of(inputs)
-    cot_own, _ = halves_of(cotangent)
-
-    z0, stats = project(plan, 0, sizes, copies, scal, x_own, x_other, pieces)
+        whole = both(blocks_of(whole.reshape(total, total), width), True)
+        pieces0, pieces1 = [whole[0]], [whole[1]]
+        plan, shapes = WHOLE, [(2 * HALF, HALF)]
+
+    def turned_over(x):
+        return x.transpose(0, 1, 3, 2).reshape(micro * views, total, frames)
+
+    x_own, x_other = spread(scal, turned_over(inputs), 2)
+    (cot_own,) = spread(scal, turned_over(cotangent), 1)
+
+    z0, stats = project(plan, sizes, copies, scal, x_own, x_other, pieces0)
     y1_own, h0, norm0 = forward(sizes, scal, totals, exchange(stats), par[0], z0, x_own)
     y1_other = swap(y1_own)
-    z1, stats = project(plan, 1, sizes, copies, scal, y1_own, y1_other, pieces)
+    z1, stats = project(WHOLE, sizes, copies, scal, y1_own, y1_other, pieces1)
     y2_own, p1, sums1, norm1 = turn(
         sizes, copies, scal, totals, exchange(stats), par[1], z1, y1_own, cot_own
     )
     sums1 = exchange(sums1)
-    dz1, mine, theirs = unproject(plan, 1, sizes, scal, totals, sums1, par[1], norm1, z1, p1, pieces)
+    dz1, mine, theirs = unproject(WHOLE, sizes, scal, totals, sums1, par[1], norm1, z1, p1, pieces1)
     theirs = swap(theirs)
-    cut, shapes = scatter_plan() if routed else ([(0, (), None, 0, 2 * HALF)], [(2 * HALF, HALF)])
     kind = BF16 if routed else F32
-    dw1 = outer(cut, shapes, kind, scal, y1_own, y1_other, dz1)
+    (dw1,) = outer(WHOLE, [(2 * HALF, HALF)], kind, scal, y1_own, y1_other, dz1)
+    if routed:
+        dw1 = lax.psum_scatter(dw1.reshape(2 * SUB, LANES, HALF), "dp")
     g1_own, p0, sums0 = backward(sizes, copies, scal, par[0], norm0, z0, h0, cot_own, mine, theirs)
     sums0 = exchange(sums0)
-    dz0, mine, theirs = unproject(plan, 0, sizes, scal, totals, sums0, par[0], norm0, z0, p0, pieces)
+    dz0, mine, theirs = unproject(plan, sizes, scal, totals, sums0, par[0], norm0, z0, p0, pieces0)
     theirs = swap(theirs)
-    dw0 = outer(cut, shapes, kind, scal, x_own, x_other, dz0)
-    g0_own = (g1_own.astype(F32) + (mine + theirs)).astype(BF16)
+    dw0 = outer(plan, shapes, kind, scal, x_own, x_other, dz0)
+    g0_own, sent = finish(scal, g1_own, mine, theirs, frames)
+    got = swap(sent)
+    y2_low = lax.ppermute(y2_own, "section", [(0, 1)])
+
+    def turned_back(halves):
+        out = join(scal, halves, total, frames)
+        return out.reshape(1, micro, views, total, frames).transpose(0, 1, 2, 4, 3)
+
+    activations = turned_back((y1_own, y1_other, y2_low, y2_own))
+    input_grads = turned_back((g0_own, got, got, g1_own))
 
     if routed:
-        grads = jnp.stack([scatter_pieces(dw0), scatter_pieces(dw1)])
-        own, other = both(grads, False)[0], swap(lax.dynamic_index_in_dim(grads, 1 - section, 0, keepdims=False))
-        weight_grads = join(scal, own, other, total, LANES)[:width].reshape(1, entries)
+        dw0, activations, input_grads = scatter_pieces(dw0, activations, input_grads)
+        rows_of = natural_rows(scal, *both(jnp.stack([dw0, dw1.astype(F32)]), False), total)
+        weight_grads = rows_of[:width].reshape(1, entries)
     else:
-        grads = jnp.stack([dw0[0], dw1[0]])
-        own, other = both(grads, False)
-        square = join(scal, own, other, total, LANES).reshape(2 * SUB, LANES, total)[:, :width]
-        weight_grads = lax.psum_scatter(square.reshape(1, -1), "dp", scatter_dimension=1, tiled=True)
-
-    shape = (1, micro, views, frames, total)
-    act_own = jnp.where(section == 0, y1_own, y2_own)
-    act_other = jnp.where(section == 0, y1_other, swap(y2_own))
-    activations = join(scal, act_own, act_other, total, frames).reshape(shape)
-    grad_own = jnp.where(section == 0, g0_own, g1_own)
-    grad_other = swap(jnp.where(section == 0, g1_own, g0_own))
-    input_grads = join(scal, grad_own, grad_other, total, frames).reshape(shape)
+        rows_of = natural_rows(scal, *both(jnp.stack([dw0[0], dw1]), False), total)
+        rows_of = rows_of.reshape(-1, LANES, total)[:, :width].reshape(1, -1)
+        weight_grads = lax.psum_scatter(rows_of, "dp", scatter_dimension=1, tiled=True)
 
     sums = [jnp.sum(s, axis=(0, 1)) for s in (sums0, sums1)]
     sums = jnp.stack(sums)[..., :width].reshape(2, 3, SUB * width)

time: 497 us -> 365 us (0.73)
  waiting for transfers between devices: 197 us -> 116 us
  Pallas kernels: 119 us -> 80 us
  other arithmetic: 39 us -> 15.1 us
  starting transfers between devices: 75.6 us -> 54.5 us
  blocking collectives: 16.5 us -> 35.9 us
  between operations: 1.51 us -> 15.1 us
    ppermute x39 -> x26, waiting for transfers between devices: 190 us -> 83.2 us  [flip(): return lax.ppermute(x, 'dp', [(i, i ^ mask) for i in range(count)])]
    pallas_call x10 -> x11, Pallas kernels: 74.3 us -> 50.6 us  [the longest x2 16.5 us: unproject(): pl.pallas_call(partial(unproject_kernel, plan, sizes), in_specs=[SMEM, SM...]
    all_to_all x1 -> x2, blocking collectives: 16.5 us -> 35.9 us  [exchange(): return lax.all_to_all(x, 'dp', 0, 0)]
    all_to_all x3 -> x2, waiting for transfers between devices: 2.06 us -> 15.4 us  [exchange(): return lax.all_to_all(x, 'dp', 0, 0)]
    reduce_scatter x0 -> x1, waiting for transfers between devices: none -> 12.8 us  [per_device(): dw1 = lax.psum_scatter(dw1.reshape(2 * SUB, LANES, HALF), 'dp')]
    unnamed x1 -> x0, other arithmetic: 11.4 us -> none
    ppermute x9 -> x8, starting transfers between devices: 23.5 us -> 12.2 us  [swap(): return lax.ppermute(x, 'section', [(0, 1), (1, 0)])]
    unnamed x79 -> x139, local copies, waits for them, and re-layouts: 23.7 us -> 34.9 us
  transfers between devices with their start and end apart: 51 -> 39, of which waited for: 27 -> 20; matrix products, arithmetic and copies ran while one was open for 12% -> 4% of each run, Pallas kernels for 13% -> 15%
where the time goes in v2:
time: 365 us; the launch traced here: 358 us
  waiting for transfers between devices  116 us (32%)
  Pallas kernels  80 us (22%)
  starting transfers between devices  54.5 us (15%)
  local copies, waits for them, and re-layouts  41.6 us (11%)
  blocking collectives  35.9 us (10%)
  other arithmetic  15.1 us (4%)
  between operations  15.1 us (4%)
    ppermute x26, waiting for transfers between devices, flip(): return lax.ppermute(x, 'dp', [(i, i ^ mask) for i in range(count)])  83.2 us
    all_to_all x2, blocking collectives, exchange(): return lax.all_to_all(x, 'dp', 0, 0)  35.9 us
    unnamed x139, local copies, waits for them, and re-layouts  34.9 us
    ppermute x26, starting transfers between devices, flip(): return lax.ppermute(x, 'dp', [(i, i ^ mask) for i in range(count)])  23.9 us
    all_to_all x2, starting transfers between devices, exchange(): return lax.all_to_all(x, 'dp', 0, 0)  17 us
    pallas_call x2, Pallas kernels, unproject(): pl.pallas_call(partial(unproject_kernel, plan, sizes), in_specs=[SMEM, SM...  16.5 us
    all_to_all x2, waiting for transfers between devices, exchange(): return lax.all_to_all(x, 'dp', 0, 0)  15.4 us
    pallas_call x2, Pallas kernels, project(): pl.pallas_call(partial(project_kernel, plan, sizes), in_specs=[SMEM, VMEM...  13.3 us
  transfers between devices with their start and end apart: 39, of which 20 were waited for; matrix products, arithmetic and copies ran while one was open for 4% of the time, Pallas kernels for 15%

profile of v2, /device:TPU:19, one launch (start us, length us, event | category | flops | bytes accessed | tf_op | source)
XLA Modules:
  0.0 358.5 jit_solution(4049054612725888571)
XLA Ops:
  8.4 2.3 cut.1
  17.7 2.9 collective-permute-done.7
  21.3 2.7 collective-permute-done.5
  24.0 9.9 %collective-permute-done.4 = bf16[96,1024]{1,0:T(8,128)(2,1)S(1)} collective-permute-done((bf16[96,1024]{1,0:T(8,128)(2,1)S(1)}, bf16[96,1024]{1,0:T(8,128)(2,1)S(1)}, u32[]{:S(2)}, u32[]{:S(2)}) %collective-permute-start.4) | collective-permute-done | bytes 196640 | tf_op jit(solution)/shard_map/ppermute | solution.py:592
  35.7 8.5 %collective-permute-done.10 = bf16[2,96,1024]{2,1,0:T(8,128)(2,1)S(1)} collective-permute-done((bf16[2,96,1024]{2,1,0:T(8,128)(2,1)S(1)}, bf16[2,96,1024]{2,1,0:T(8,128)(2,1)S(1)}, u32[]{:S(2)}, u32[]{:S(2)}) %collective-permute-start.10) | collective-permute-done | bytes 393248 | tf_op jit(solution)/shard_map/ppermute | solution.py:592
  44.3 2.0 pad_maximum_fusion.1.rest_2_
  49.9 2.6 collective-permute-start.12
  53.5 2.3 spread.2
  55.9 13.0 %collective-permute-done.14.rest_7_ = bf16[4,32,1024]{2,1,0:T(8,128)(2,1)} collective-permute-done((bf16[4,32,1024]{2,1,0:T(8,128)(2,1)S(1)}, bf16[4,32,1024]{2,1,0:T(8,128)(2,1)}, u32[]{:S(2)}, u32[]{:S(2)}) %collective-permute-start.14) | collective-permute-done | bytes 262176 | tf_op jit(solution)/shard_map/ppermute | solution.py:592
  68.9 7.7 %collective-permute-done.13.rest_6_ = bf16[4,32,1024]{2,1,0:T(8,128)(2,1)} collective-permute-done((bf16[4,32,1024]{2,1,0:T(8,128)(2,1)S(1)}, bf16[4,32,1024]{2,1,0:T(8,128)(2,1)}, u32[]{:S(2)}, u32[]{:S(2)}) %collective-permute-start.13) | collective-permute-done | bytes 262176 | tf_op jit(solution)/shard_map/ppermute | solution.py:592
  76.6 7.4 %project.2 = (f32[6144,128]{1,0:T(8,128)S(1)}, f32[16,2,2,8,128]{4,3,2,1,0:T(8,128)S(1)}) custom-call(s32[4]{0:T(128)S(1)} %pad_add_fusion.scal, bf16[768,1024]{1,0:T(8,128)(2,1)S(1)} %get-tuple-element.57.own_ref.v_ref, bf16[768,1024]{1,0:T(8,128)(2,1)S(1)} %get-tuple-element.58.other_ref, bf16[4,96,1024]{2,1,0:T(8,128)(2,1)} %pad_maximum_fusion.rest_0_, ...), custom_call_target="tpu_custom_call" | custom-call | flops 3221225472 | bytes 12582912 | tf_op jit(solution)/shard_map/project/pallas_call | solution.py:273
  84.7 11.4 %all-to-all-start = ((f32[16,2,2,8,128]{4,3,2,1,0:T(8,128)}), f32[16,2,2,8,128]{4,3,2,1,0:T(8,128)S(1)}, u32[]{:S(2)}, u32[]{:S(2)}) async-start(f32[16,2,2,8,128]{4,3,2,1,0:T(8,128)} %copy-done.38), calls=%async_computation | async-start | bytes 524288 | tf_op jit(solution)/shard_map/all_to_all | solution.py:653
  96.1 2.0 collective-permute-start
  99.0 11.7 %all-to-all-done.stats_ref = f32[16,2,2,8,128]{4,3,2,1,0:T(8,128)S(1)} async-done(((f32[16,2,2,8,128]{4,3,2,1,0:T(8,128)}), f32[16,2,2,8,128]{4,3,2,1,0:T(8,128)S(1)}, u32[]{:S(2)}, u32[]{:S(2)}) %all-to-all-start) | async-done | bytes 262176 | tf_op jit(solution)/shard_map/all_to_all | solution.py:653
  112.1 3.5 forward.1
  117.9 2.6 collective-permute-start.15
  121.6 1.9 collective-permute-done.15.other_ref.rest_1_
  123.5 2.0 copy-done.4
  125.5 2.2 copy-done.47
  127.7 5.9 %project.3 = (f32[6144,128]{1,0:T(8,128)S(1)}, f32[16,2,2,8,128]{4,3,2,1,0:T(8,128)}) custom-call(s32[4]{0:T(128)S(1)} %pad_add_fusion.scal, bf16[768,1024]{1,0:T(8,128)(2,1)S(1)} %copy-done.4, bf16[768,1024]{1,0:T(8,128)(2,1)S(1)} %collective-permute-done.15.other_ref.rest_1_, bf16[2048,1024]{1,0:T(8,128)(2,1)S(1)} %copy-done.47), custom_call_target="tpu_custom_call" | custom-call | flops 3221225472 | bytes 12582912 | tf_op jit(solution)/shard_map/project/pallas_call | solution.py:273
  135.3 5.6 %all-to-all-start.1 = ((f32[16,2,2,8,128]{4,3,2,1,0:T(8,128)}), f32[16,2,2,8,128]{4,3,2,1,0:T(8,128)S(1)}, u32[]{:S(2)}, u32[]{:S(2)}) async-start(f32[16,2,2,8,128]{4,3,2,1,0:T(8,128)} %get-tuple-element.71), calls=%async_computation.1 | async-start | bytes 524288 | tf_op jit(solution)/shard_map/all_to_all | solution.py:653
  142.7 1.9 spread.3.cot_ref.base_ref
  144.6 3.7 %all-to-all-done.1.stats_ref = f32[16,2,2,8,128]{4,3,2,1,0:T(8,128)S(1)} async-done(((f32[16,2,2,8,128]{4,3,2,1,0:T(8,128)}), f32[16,2,2,8,128]{4,3,2,1,0:T(8,128)S(1)}, u32[]{:S(2)}, u32[]{:S(2)}) %all-to-all-start.1) | async-done | bytes 262176 | tf_op jit(solution)/shard_map/all_to_all | solution.py:653
  148.4 1.9 copy-done.12
  150.2 6.7 %turn.1 = (bf16[768,1024]{1,0:T(8,128)(2,1)S(1)}, f32[6144,128]{1,0:T(8,128)S(1)}, f32[16,2,3,8,128]{4,3,2,1,0:T(8,128)S(1)}, f32[2,2,8,128]{3,2,1,0:T(8,128)S(1)}) custom-call(s32[4]{0:T(128)S(1)} %pad_add_fusion.scal, f32[2]{0:T(128)S(1)} %convert_multiply_fusion.totals, f32[16,2,2,8,128]{4,3,2,1,0:T(8,128)S(1)} %all-to-all-done.1.stats_ref, ...), custom_call_target="tpu_custom_call" | custom-call | flops 15728640 | bytes 11010048 | tf_op jit(solution)/shard_map/turn/pallas_call | solution.py:437
  158.1 15.6 %all_to_all.20.sums_ref = f32[16,2,3,8,128]{4,3,2,1,0:T(8,128)S(1)} all-to-all(f32[16,2,3,8,128]{4,3,2,1,0:T(8,128)S(1)} %get-tuple-element.73), channel_id=1, replica_groups=mesh['section'=2,'dp'=16] {'dp'}, dimensions={0} | all-to-all | bytes 786432 | tf_op jit(solution)/shard_map/all_to_all | solution.py:653
  175.0 8.6 %unproject.2 = (bf16[768,1024]{1,0:T(8,128)(2,1)S(1)}, f32[768,1024]{1,0:T(8,128)S(1)}, f32[768,1024]{1,0:T(8,128)}) custom-call(s32[4]{0:T(128)S(1)} %pad_add_fusion.scal, f32[2]{0:T(128)S(1)} %copy-done.45, f32[16,2,3,8,128]{4,3,2,1,0:T(8,128)S(1)} %all_to_all.20.sums_ref, f32[3,8,128]{2,1,0:T(8,128)S(1)} %copy-done.40, ...), custom_call_target="tpu_custom_call" | custom-call | flops 3221225472 | bytes 25165824 | tf_op jit(solution)/shard_map/unproject/pallas_call | solution.py:531
  185.2 4.4 %outer.3 = bf16[2048,1024]{1,0:T(8,128)(2,1)S(1)} custom-call(s32[4]{0:T(128)S(1)} %pad_add_fusion.scal, bf16[768,1024]{1,0:T(8,128)(2,1)S(1)} %copy-done.5, bf16[768,1024]{1,0:T(8,128)(2,1)S(1)} %copy-done.22, bf16[768,1024]{1,0:T(8,128)(2,1)S(1)} %get-tuple-element.107.dz_ref), custom_call_target="tpu_custom_call" | custom-call | flops 3221225472 | bytes 12582912 | tf_op jit(solution)/shard_map/outer/pallas_call | solution.py:573
  189.6 2.0 copy-done.8
  193.5 1.9 copy-done.10
  195.4 1.9 copy-done.15
  198.0 7.0 %backward.1 = (bf16[768,1024]{1,0:T(8,128)(2,1)S(1)}, f32[6144,128]{1,0:T(8,128)S(1)}, f32[16,2,3,8,128]{4,3,2,1,0:T(8,128)S(1)}) custom-call(s32[4]{0:T(128)S(1)} %pad_add_fusion.scal, f32[3,8,128]{2,1,0:T(8,128)S(1)} %get-tuple-element.122.par_ref, f32[2,2,8,128]{3,2,1,0:T(8,128)S(1)} %copy-done.42, f32[6144,128]{1,0:T(8,128)S(1)} %copy-done.1, ...), custom_call_target="tpu_custom_call" | custom-call | flops 15728640 | bytes 18874368 | tf_op jit(solution)/shard_map/backward/pallas_call | solution.py:479
  205.1 20.3 %all_to_all.21.sums_ref = f32[16,2,3,8,128]{4,3,2,1,0:T(8,128)S(1)} all-to-all(f32[16,2,3,8,128]{4,3,2,1,0:T(8,128)S(1)} %get-tuple-element.78), channel_id=1, replica_groups=mesh['section'=2,'dp'=16] {'dp'}, dimensions={0} | all-to-all | bytes 786432 | tf_op jit(solution)/shard_map/all_to_all | solution.py:653
  225.5 7.9 %unproject.3 = (bf16[768,1024]{1,0:T(8,128)(2,1)S(1)}, f32[768,1024]{1,0:T(8,128)S(1)}, f32[768,1024]{1,0:T(8,128)S(1)}) custom-call(s32[4]{0:T(128)S(1)} %pad_add_fusion.scal, f32[2]{0:T(128)S(1)} %copy-done.46, f32[16,2,3,8,128]{4,3,2,1,0:T(8,128)S(1)} %all_to_all.21.sums_ref, f32[3,8,128]{2,1,0:T(8,128)S(1)} %get-tuple-element.122.par_ref, ...), custom_call_target="tpu_custom_call" | custom-call | flops 3221225472 | bytes 25165824 | tf_op jit(solution)/shard_map/unproject/pallas_call | solution.py:531
  235.7 7.9 %outer.2 = (bf16[4,96,1024]{2,1,0:T(8,128)(2,1)S(1)}, bf16[4,96,1024]{2,1,0:T(8,128)(2,1)}, bf16[4,96,1024]{2,1,0:T(8,128)(2,1)S(1)}, bf16[4,96,1024]{2,1,0:T(8,...) custom-call(s32[4]{0:T(128)S(1)} %pad_add_fusion.scal, ...), custom_call_target="tpu_custom_call" | custom-call | flops 3221225472 | bytes 12582912 | tf_op jit(solution)/shard_map/outer/pallas_call | solution.py:573
  245.5 3.1 finish.1
  249.8 2.1 collective-permute-start.29
  253.0 2.0 collective-permute-start.18
  260.1 4.1 %join.2 = bf16[6,2000,128]{2,1,0:T(8,128)(2,1)} custom-call(s32[4]{0:T(128)S(1)} %pad_add_fusion.scal, bf16[768,1024]{1,0:T(8,128)(2,1)S(1)} %copy-done.5, bf16[768,1024]{1,0:T(8,128)(2,1)S(1)} %copy-done.23, bf16[768,1024]{1,0:T(8,128)(2,1)S(1)} %copy-done.30, bf16[768,1024]{1,0:T(8,128)(2,1)S(1)} %copy-done.26), custom_call_target="tpu_custom_call" | custom-call | tf_op jit(solution)/shard_map/join/pallas_call | solution.py:138
  264.8 7.4 %collective-permute-done.18 = bf16[4,32,1024]{2,1,0:T(8,128)(2,1)} collective-permute-done((bf16[4,32,1024]{2,1,0:T(8,128)(2,1)}, bf16[4,32,1024]{2,1,0:T(8,128)(2,1)}, u32[]{:S(2)}, u32[]{:S(2)}) %collective-permute-start.18) | collective-permute-done | bytes 262176 | tf_op jit(solution)/shard_map/ppermute | solution.py:592
  272.3 5.6 %collective-permute-done.19 = bf16[4,32,1024]{2,1,0:T(8,128)(2,1)} collective-permute-done((bf16[4,32,1024]{2,1,0:T(8,128)(2,1)}, bf16[4,32,1024]{2,1,0:T(8,128)(2,1)}, u32[]{:S(2)}, u32[]{:S(2)}) %collective-permute-start.19) | collective-permute-done | bytes 262176 | tf_op jit(solution)/shard_map/ppermute | solution.py:592
  277.9 9.1 %collective-permute-done.21 = bf16[4,96,1024]{2,1,0:T(8,128)(2,1)} collective-permute-done((bf16[4,96,1024]{2,1,0:T(8,128)(2,1)}, bf16[4,96,1024]{2,1,0:T(8,128)(2,1)}, u32[]{:S(2)}, u32[]{:S(2)}) %collective-permute-start.21) | collective-permute-done | bytes 786464 | tf_op jit(solution)/shard_map/ppermute | solution.py:592
  293.0 3.2 collective-permute-start.23
  301.5 12.8 %reduce-scatter.2.cloned.1.call-done = bf16[1,128,1024]{2,1,0:T(8,128)(2,1)} async-done(((bf16[16,128,1024]{2,1,0:T(8,128)(2,1)}), bf16[1,128,1024]{2,1,0:T(8,128)(2,1)}) %reduce-scatter.2.cloned.1.call-update) | async-done | bytes 262160 | tf_op jit(solution)/shard_map/reduce_scatter | solution.py:718
  315.3 6.0 %join.3 = bf16[6,2000,128]{2,1,0:T(8,128)(2,1)} custom-call(s32[4]{0:T(128)S(1)} %pad_add_fusion.scal, bf16[768,1024]{1,0:T(8,128)(2,1)S(1)} %copy-done.28, bf16[768,1024]{1,0:T(8,128)(2,1)} %collective-permute-done.29.rest_1_.rest_2_, bf16[768,1024]{1,0:T(8,128)(2,1)} %collective-permute-done.29.rest_1_.rest_2_, bf16[768,1024]{1,0:T(8,128)(2,1)S(1)} %copy-done.7), custom_call_target="tpu_custom_call" | custom-call | tf_op jit(solution)/shard_map/join/pallas_call | solution.py:138
  327.4 2.2 collective-permute-done.30
  330.7 12.5 %collective-permute-done.32 = bf16[96,1024]{1,0:T(8,128)(2,1)S(1)} collective-permute-done((bf16[96,1024]{1,0:T(8,128)(2,1)S(1)}, bf16[96,1024]{1,0:T(8,128)(2,1)S(1)}, u32[]{:S(2)}, u32[]{:S(2)}) %collective-permute-start.32) | collective-permute-done | bytes 196640 | tf_op jit(solution)/shard_map/ppermute | solution.py:592
  348.8 2.6 reshape.54
  (229 shorter events, 69.0 us)
Async XLA Ops:
  7.2 116.4 %all-gather.3.cloned.1.call-start = ((), (), s32[]{:S(2)}) async-start(), calls=%async_computation.6 | async-start | bytes 4456448 | tf_op jit(solution)/shard_map/all_gather | solution.py:691
  10.8 1.9 collective-permute-start.1
  13.5 10.5 %collective-permute-start.3 = (bf16[96,1024]{1,0:T(8,128)(2,1)S(1)}, bf16[96,1024]{1,0:T(8,128)(2,1)S(1)}, u32[]{:S(2)}, u32[]{:S(2)}) collective-permute-start(bf16[96,1024]{1,0:T(8,128)(2,1)S(1)} %get-tuple-element.120), channel_id=1, source_target_pairs={{0,8},{1,9},{2,10},{3,11},{4,12},{5,13},{6,14},{7,15},{8,0},{9,1},... | collective-permute-start | bytes 589832 | tf_op jit(solution)/shard_map/ppermute | solution.py:592
  13.6 10.4 %collective-permute-start.2 = (bf16[96,1024]{1,0:T(8,128)(2,1)S(1)}, bf16[96,1024]{1,0:T(8,128)(2,1)S(1)}, u32[]{:S(2)}, u32[]{:S(2)}) collective-permute-start(bf16[96,1024]{1,0:T(8,128)(2,1)S(1)} %get-tuple-element.120), channel_id=1, source_target_pairs={{0,4},{1,5},{2,6},{3,7},{4,0},{5,1},{6,2},{7,3},{8,12},{9,13},{10,... | collective-permute-start | bytes 589832 | tf_op jit(solution)/shard_map/ppermute | solution.py:592
  14.9 19.0 %collective-permute-start.4 = (bf16[96,1024]{1,0:T(8,128)(2,1)S(1)}, bf16[96,1024]{1,0:T(8,128)(2,1)S(1)}, u32[]{:S(2)}, u32[]{:S(2)}) collective-permute-start(bf16[96,1024]{1,0:T(8,128)(2,1)S(1)} %get-tuple-element.120), channel_id=1, source_target_pairs={{0,12},{1,13},{2,14},{3,15},{4,8},{5,9},{6,10},{7,11},{8,4},{9,5},... | collective-permute-start | bytes 589832 | tf_op jit(solution)/shard_map/ppermute | solution.py:592
  16.2 4.4 %collective-permute-start.7 = (bf16[32,1024]{1,0:T(8,128)(2,1)S(1)}, bf16[32,1024]{1,0:T(8,128)(2,1)S(1)}, u32[]{:S(2)}, u32[]{:S(2)}) collective-permute-start(bf16[32,1024]{1,0:T(8,128)(2,1)S(1)} %get-tuple-element.118), channel_id=1, source_target_pairs={{0,3},{1,2},{2,1},{3,0},{4,7},{5,6},{6,5},{7,4},{8,11},{9,10},{10,... | collective-permute-start | bytes 196616 | tf_op jit(solution)/shard_map/ppermute | solution.py:592
  17.5 3.8 %collective-permute-start.6 = (bf16[32,1024]{1,0:T(8,128)(2,1)S(1)}, bf16[32,1024]{1,0:T(8,128)(2,1)S(1)}, u32[]{:S(2)}, u32[]{:S(2)}) collective-permute-start(bf16[32,1024]{1,0:T(8,128)(2,1)S(1)} %get-tuple-element.118), channel_id=1, source_target_pairs={{0,2},{1,3},{2,0},{3,1},{4,6},{5,7},{6,4},{7,5},{8,10},{9,11},{10,... | collective-permute-start | bytes 196616 | tf_op jit(solution)/shard_map/ppermute | solution.py:592
  20.6 3.4 collective-permute-start.5
  34.0 10.3 %collective-permute-start.10 = (bf16[2,96,1024]{2,1,0:T(8,128)(2,1)S(1)}, bf16[2,96,1024]{2,1,0:T(8,128)(2,1)S(1)}, u32[]{:S(2)}, u32[]{:S(2)}) collective-permute-start(bf16[2,96,1024]{2,1,0:T(8,128)(2,1)S(1)} %pad_maximum_fusion.3), channel_id=1, source_target_pairs={{0,2},{1,3},{2,0},{3,1},{4,6},{5,7},{6,4},{7,5},{8,10},{9,11},{10,... | collective-permute-start | bytes 1179656 | tf_op jit(solution)/shard_map/ppermute | solution.py:592
  35.4 11.1 %collective-permute-start.8 = (bf16[2,96,1024]{2,1,0:T(8,128)(2,1)S(1)}, bf16[2,96,1024]{2,1,0:T(8,128)(2,1)S(1)}, u32[]{:S(2)}, u32[]{:S(2)}) collective-permute-start(bf16[2,96,1024]{2,1,0:T(8,128)(2,1)S(1)} %pad_maximum_fusion.2), channel_id=1, source_target_pairs={{0,1},{1,0},{2,3},{3,2},{4,5},{5,4},{6,7},{7,6},{8,9},{9,8},{10,11... | collective-permute-start | bytes 1179656 | tf_op jit(solution)/shard_map/ppermute | solution.py:592
  46.3 30.2 %collective-permute-start.11 = (bf16[4,96,1024]{2,1,0:T(8,128)(2,1)}, bf16[4,96,1024]{2,1,0:T(8,128)(2,1)}, u32[]{:S(2)}, u32[]{:S(2)}) collective-permute-start(bf16[4,96,1024]{2,1,0:T(8,128)(2,1)} %pad_maximum_fusion.1.rest_2_), channel_id=1, source_target_pairs={{0,1},{1,0},{2,3},{3,2},{4,5},{5,4},{6,7},{7,6},{8,9},{9,8},{10,11... | collective-permute-start | bytes 2359304 | tf_op jit(solution)/shard_map/ppermute | solution.py:592
  47.5 29.0 %collective-permute-start.9 = (bf16[4,96,1024]{2,1,0:T(8,128)(2,1)}, bf16[4,96,1024]{2,1,0:T(8,128)(2,1)}, u32[]{:S(2)}, u32[]{:S(2)}) collective-permute-start(bf16[4,96,1024]{2,1,0:T(8,128)(2,1)} %pad_maximum_fusion.rest_0_), channel_id=1, source_target_pairs={{0,2},{1,3},{2,0},{3,1},{4,6},{5,7},{6,4},{7,5},{8,10},{9,11},{10,... | collective-permute-start | bytes 2359304 | tf_op jit(solution)/shard_map/ppermute | solution.py:592
  49.7 19.2 %collective-permute-start.14 = (bf16[4,32,1024]{2,1,0:T(8,128)(2,1)S(1)}, bf16[4,32,1024]{2,1,0:T(8,128)(2,1)}, u32[]{:S(2)}, u32[]{:S(2)}) collective-permute-start(bf16[4,32,1024]{2,1,0:T(8,128)(2,1)S(1)} %pad_maximum_fusion.4.rest_4_), channel_id=1, source_target_pairs={{0,12},{1,13},{2,14},{3,15},{4,8},{5,9},{6,10},{7,11},{8,4},{9,5},... | collective-permute-start | bytes 786440 | tf_op jit(solution)/shard_map/ppermute | solution.py:592
  49.8 26.8 %collective-permute-start.13 = (bf16[4,32,1024]{2,1,0:T(8,128)(2,1)S(1)}, bf16[4,32,1024]{2,1,0:T(8,128)(2,1)}, u32[]{:S(2)}, u32[]{:S(2)}) collective-permute-start(bf16[4,32,1024]{2,1,0:T(8,128)(2,1)S(1)} %pad_maximum_fusion.4.rest_4_), channel_id=1, source_target_pairs={{0,8},{1,9},{2,10},{3,11},{4,12},{5,13},{6,14},{7,15},{8,0},{9,1},... | collective-permute-start | bytes 786440 | tf_op jit(solution)/shard_map/ppermute | solution.py:592
  49.9 26.7 %collective-permute-start.12 = (bf16[4,32,1024]{2,1,0:T(8,128)(2,1)S(1)}, bf16[4,32,1024]{2,1,0:T(8,128)(2,1)}, u32[]{:S(2)}, u32[]{:S(2)}) collective-permute-start(bf16[4,32,1024]{2,1,0:T(8,128)(2,1)S(1)} %pad_maximum_fusion.4.rest_4_), channel_id=1, source_target_pairs={{0,4},{1,5},{2,6},{3,7},{4,0},{5,1},{6,2},{7,3},{8,12},{9,13},{10,... | collective-permute-start | bytes 786440 | tf_op jit(solution)/shard_map/ppermute | solution.py:592
  55.9 28.1 %copy-start.18 = (bf16[768,1024]{1,0:T(8,128)(2,1)}, bf16[768,1024]{1,0:T(8,128)(2,1)S(1)}, u32[]{:S(2)}) copy-start(bf16[768,1024]{1,0:T(8,128)(2,1)S(1)} %get-tuple-element.57.own_ref.v_ref) | copy-start | bytes 4718596
  55.9 28.1 %copy-start.49 = (bf16[768,1024]{1,0:T(8,128)(2,1)}, bf16[768,1024]{1,0:T(8,128)(2,1)S(1)}, u32[]{:S(2)}) copy-start(bf16[768,1024]{1,0:T(8,128)(2,1)S(1)} %get-tuple-element.58.other_ref) | copy-start | bytes 4718596
  84.7 30.9 %copy-start = (f32[6144,128]{1,0:T(8,128)}, f32[6144,128]{1,0:T(8,128)S(1)}, u32[]{:S(2)}) copy-start(f32[6144,128]{1,0:T(8,128)S(1)} %get-tuple-element.66.z_ref) | copy-start | bytes 9437188
  84.7 26.0 %all-to-all-start = ((f32[16,2,2,8,128]{4,3,2,1,0:T(8,128)}), f32[16,2,2,8,128]{4,3,2,1,0:T(8,128)S(1)}, u32[]{:S(2)}, u32[]{:S(2)}) async-start(f32[16,2,2,8,128]{4,3,2,1,0:T(8,128)} %copy-done.38), calls=%async_computation | async-start | bytes 524288 | tf_op jit(solution)/shard_map/all_to_all | solution.py:653
  96.1 2.8 collective-permute-start
  98.3 50.0 %copy-start.44 = (f32[2]{0:T(128)}, f32[2]{0:T(128)S(1)}, u32[]{:S(2)}) copy-start(f32[2]{0:T(128)S(1)} %convert_multiply_fusion.totals) | copy-start | bytes 28
  99.0 49.3 %copy-start.39 = (f32[3,8,128]{2,1,0:T(8,128)}, f32[3,8,128]{2,1,0:T(8,128)S(1)}, u32[]{:S(2)}) copy-start(f32[3,8,128]{2,1,0:T(8,128)S(1)} %get-tuple-element.121.par_ref) | copy-start | bytes 36868
  117.9 5.6 %collective-permute-start.15 = (bf16[768,1024]{1,0:T(8,128)(2,1)S(1)}, bf16[768,1024]{1,0:T(8,128)(2,1)S(1)}, u32[]{:S(2)}, u32[]{:S(2)}) collective-permute-start(bf16[768,1024]{1,0:T(8,128)(2,1)S(1)} %get-tuple-element.69.own_ref.v_ref.rest_0_), channel_id=1, source_target_pairs={{0,16},{16,0},{1,17},{17,1},{2,18},{18,2},{3,19},{19,3},{4,20},{20... | collective-permute-start | bytes 4718600 | tf_op jit(solution)/shard_map/ppermute | solution.py:596
  135.3 13.1 %all-to-all-start.1 = ((f32[16,2,2,8,128]{4,3,2,1,0:T(8,128)}), f32[16,2,2,8,128]{4,3,2,1,0:T(8,128)S(1)}, u32[]{:S(2)}, u32[]{:S(2)}) async-start(f32[16,2,2,8,128]{4,3,2,1,0:T(8,128)} %get-tuple-element.71), calls=%async_computation.1 | async-start | bytes 524288 | tf_op jit(solution)/shard_map/all_to_all | solution.py:653
  140.8 173.5 %reduce-scatter.2.cloned.1.call-start = ((), (), s32[]{:S(2)}) async-start(), calls=%async_computation.5 | async-start | bytes 4456448 | tf_op jit(solution)/shard_map/reduce_scatter | solution.py:718
  183.6 8.1 %collective-permute-start.16 = (f32[768,1024]{1,0:T(8,128)}, f32[768,1024]{1,0:T(8,128)}, u32[]{:S(2)}, u32[]{:S(2)}) collective-permute-start(f32[768,1024]{1,0:T(8,128)} %get-tuple-element.77), channel_id=1, source_target_pairs={{0,16},{16,0},{1,17},{17,1},{2,18},{18,2},{3,19},{19,3},{4,20},{20... | collective-permute-start | bytes 9437192 | tf_op jit(solution)/shard_map/ppermute | solution.py:596
  198.0 27.4 %copy-start.37 = (bf16[4,32,1024]{2,1,0:T(8,128)(2,1)S(1)}, bf16[4,32,1024]{2,1,0:T(8,128)(2,1)}, u32[]{:S(2)}) copy-start(bf16[4,32,1024]{2,1,0:T(8,128)(2,1)} %copy-done.36) | copy-start | bytes 786436
  198.0 27.4 %copy-start.43 = (f32[2,2,8,128]{3,2,1,0:T(8,128)S(1)}, f32[2,2,8,128]{3,2,1,0:T(8,128)}, u32[]{:S(2)}) copy-start(f32[2,2,8,128]{3,2,1,0:T(8,128)} %copy-done.41) | copy-start | bytes 49156
  198.0 27.4 %copy-start.46 = (f32[2]{0:T(128)S(1)}, f32[2]{0:T(128)}, u32[]{:S(2)}) copy-start(f32[2]{0:T(128)} %copy-done.44) | copy-start | bytes 28
  205.1 40.5 %copy-start.6 = (bf16[768,1024]{1,0:T(8,128)(2,1)}, bf16[768,1024]{1,0:T(8,128)(2,1)S(1)}, u32[]{:S(2)}) copy-start(bf16[768,1024]{1,0:T(8,128)(2,1)S(1)} %get-tuple-element.96.g_ref.rest_3_) | copy-start | bytes 4718596
  233.4 12.1 %collective-permute-start.28 = (f32[768,1024]{1,0:T(8,128)S(1)}, f32[768,1024]{1,0:T(8,128)S(1)}, u32[]{:S(2)}, u32[]{:S(2)}) collective-permute-start(f32[768,1024]{1,0:T(8,128)S(1)} %get-tuple-element.98), channel_id=1, source_target_pairs={{0,16},{16,0},{1,17},{17,1},{2,18},{18,2},{3,19},{19,3},{4,20},{20... | collective-permute-start | bytes 9437192 | tf_op jit(solution)/shard_map/ppermute | solution.py:596
  234.4 17.5 %collective-permute-start.22 = (bf16[768,1024]{1,0:T(8,128)(2,1)S(1)}, bf16[768,1024]{1,0:T(8,128)(2,1)S(1)}, u32[]{:S(2)}, u32[]{:S(2)}) collective-permute-start(bf16[768,1024]{1,0:T(8,128)(2,1)S(1)} %copy-done.25), channel_id=1, source_target_pairs={{0,16},{1,17},{2,18},{3,19},{4,20},{5,21},{6,22},{7,23},{8,24},{9,... | collective-permute-start | bytes 4718600 | tf_op jit(solution)/shard_map/ppermute | solution.py:726
  243.6 34.2 %collective-permute-start.20 = (bf16[4,96,1024]{2,1,0:T(8,128)(2,1)}, bf16[4,96,1024]{2,1,0:T(8,128)(2,1)}, u32[]{:S(2)}, u32[]{:S(2)}) collective-permute-start(bf16[4,96,1024]{2,1,0:T(8,128)(2,1)} %get-tuple-element.84), channel_id=1, source_target_pairs={{0,2},{1,3},{2,0},{3,1},{4,6},{5,7},{6,4},{7,5},{8,10},{9,11},{10,... | collective-permute-start | bytes 2359304 | tf_op jit(solution)/shard_map/ppermute | solution.py:592
  243.7 43.3 %collective-permute-start.21 = (bf16[4,96,1024]{2,1,0:T(8,128)(2,1)}, bf16[4,96,1024]{2,1,0:T(8,128)(2,1)}, u32[]{:S(2)}, u32[]{:S(2)}) collective-permute-start(bf16[4,96,1024]{2,1,0:T(8,128)(2,1)} %get-tuple-element.85), channel_id=1, source_target_pairs={{0,1},{1,0},{2,3},{3,2},{4,5},{5,4},{6,7},{7,6},{8,9},{9,8},{10,11... | collective-permute-start | bytes 2359304 | tf_op jit(solution)/shard_map/ppermute | solution.py:592
  243.8 11.3 %collective-permute-start.17 = (bf16[4,32,1024]{2,1,0:T(8,128)(2,1)S(1)}, bf16[4,32,1024]{2,1,0:T(8,128)(2,1)S(1)}, u32[]{:S(2)}, u32[]{:S(2)}) collective-permute-start(bf16[4,32,1024]{2,1,0:T(8,128)(2,1)S(1)} %get-tuple-element.81), channel_id=1, source_target_pairs={{0,4},{1,5},{2,6},{3,7},{4,0},{5,1},{6,2},{7,3},{8,12},{9,13},{10,... | collective-permute-start | bytes 786440 | tf_op jit(solution)/shard_map/ppermute | solution.py:592
  249.8 49.5 %collective-permute-start.29 = (bf16[768,1024]{1,0:T(8,128)(2,1)}, bf16[768,1024]{1,0:T(8,128)(2,1)}, u32[]{:S(2)}, u32[]{:S(2)}) collective-permute-start(bf16[768,1024]{1,0:T(8,128)(2,1)} %get-tuple-element.100), channel_id=1, source_target_pairs={{0,16},{16,0},{1,17},{17,1},{2,18},{18,2},{3,19},{19,3},{4,20},{20... | collective-permute-start | bytes 4718600 | tf_op jit(solution)/shard_map/ppermute | solution.py:596
  253.0 19.2 %collective-permute-start.18 = (bf16[4,32,1024]{2,1,0:T(8,128)(2,1)}, bf16[4,32,1024]{2,1,0:T(8,128)(2,1)}, u32[]{:S(2)}, u32[]{:S(2)}) collective-permute-start(bf16[4,32,1024]{2,1,0:T(8,128)(2,1)} %get-tuple-element.82), channel_id=1, source_target_pairs={{0,8},{1,9},{2,10},{3,11},{4,12},{5,13},{6,14},{7,15},{8,0},{9,1},... | collective-permute-start | bytes 786440 | tf_op jit(solution)/shard_map/ppermute | solution.py:592
  255.1 22.8 %collective-permute-start.19 = (bf16[4,32,1024]{2,1,0:T(8,128)(2,1)}, bf16[4,32,1024]{2,1,0:T(8,128)(2,1)}, u32[]{:S(2)}, u32[]{:S(2)}) collective-permute-start(bf16[4,32,1024]{2,1,0:T(8,128)(2,1)} %get-tuple-element.83), channel_id=1, source_target_pairs={{0,12},{1,13},{2,14},{3,15},{4,8},{5,9},{6,10},{7,11},{8,4},{9,5},... | collective-permute-start | bytes 786440 | tf_op jit(solution)/shard_map/ppermute | solution.py:592
  291.8 29.5 %collective-permute-start.24 = (bf16[2,96,1024]{2,1,0:T(8,128)(2,1)}, bf16[2,96,1024]{2,1,0:T(8,128)(2,1)}, u32[]{:S(2)}, u32[]{:S(2)}) collective-permute-start(bf16[2,96,1024]{2,1,0:T(8,128)(2,1)} %slice.67), channel_id=1, source_target_pairs={{0,2},{1,3},{2,0},{3,1},{4,6},{5,7},{6,4},{7,5},{8,10},{9,11},{10,... | collective-permute-start | bytes 1179656 | tf_op jit(solution)/shard_map/ppermute | solution.py:592
  293.0 28.4 %collective-permute-start.23 = (bf16[2,96,1024]{2,1,0:T(8,128)(2,1)}, bf16[2,96,1024]{2,1,0:T(8,128)(2,1)}, u32[]{:S(2)}, u32[]{:S(2)}) collective-permute-start(bf16[2,96,1024]{2,1,0:T(8,128)(2,1)} %slice.66), channel_id=1, source_target_pairs={{0,1},{1,0},{2,3},{3,2},{4,5},{5,4},{6,7},{7,6},{8,9},{9,8},{10,11... | collective-permute-start | bytes 1179656 | tf_op jit(solution)/shard_map/ppermute | solution.py:592
  298.1 23.2 %collective-permute-start.27 = (bf16[32,1024]{1,0:T(8,128)(2,1)}, bf16[32,1024]{1,0:T(8,128)(2,1)S(1)}, u32[]{:S(2)}, u32[]{:S(2)}) collective-permute-start(bf16[32,1024]{1,0:T(8,128)(2,1)} %get-tuple-element.114), channel_id=1, source_target_pairs={{0,3},{1,2},{2,1},{3,0},{4,7},{5,6},{6,5},{7,4},{8,11},{9,10},{10,... | collective-permute-start | bytes 196616 | tf_op jit(solution)/shard_map/ppermute | solution.py:592
  298.4 22.9 %collective-permute-start.26 = (bf16[32,1024]{1,0:T(8,128)(2,1)}, bf16[32,1024]{1,0:T(8,128)(2,1)}, u32[]{:S(2)}, u32[]{:S(2)}) collective-permute-start(bf16[32,1024]{1,0:T(8,128)(2,1)} %get-tuple-element.115), channel_id=1, source_target_pairs={{0,2},{1,3},{2,0},{3,1},{4,6},{5,7},{6,4},{7,5},{8,10},{9,11},{10,... | collective-permute-start | bytes 196616 | tf_op jit(solution)/shard_map/ppermute | solution.py:592
  299.3 22.0 %collective-permute-start.25 = (bf16[32,1024]{1,0:T(8,128)(2,1)}, bf16[32,1024]{1,0:T(8,128)(2,1)}, u32[]{:S(2)}, u32[]{:S(2)}) collective-permute-start(bf16[32,1024]{1,0:T(8,128)(2,1)} %get-tuple-element.116), channel_id=1, source_target_pairs={{0,1},{1,0},{2,3},{3,2},{4,5},{5,4},{6,7},{7,6},{8,9},{9,8},{10,11... | collective-permute-start | bytes 196616 | tf_op jit(solution)/shard_map/ppermute | solution.py:592
  323.7 5.8 %collective-permute-start.30 = (bf16[96,1024]{1,0:T(8,128)(2,1)S(1)}, bf16[96,1024]{1,0:T(8,128)(2,1)S(1)}, u32[]{:S(2)}, u32[]{:S(2)}) collective-permute-start(bf16[96,1024]{1,0:T(8,128)(2,1)S(1)} %slice_bitcast_fusion.2), channel_id=1, source_target_pairs={{0,4},{1,5},{2,6},{3,7},{4,0},{5,1},{6,2},{7,3},{8,12},{9,13},{10,... | collective-permute-start | bytes 589832 | tf_op jit(solution)/shard_map/ppermute | solution.py:592
  325.0 5.8 %collective-permute-start.31 = (bf16[96,1024]{1,0:T(8,128)(2,1)S(1)}, bf16[96,1024]{1,0:T(8,128)(2,1)S(1)}, u32[]{:S(2)}, u32[]{:S(2)}) collective-permute-start(bf16[96,1024]{1,0:T(8,128)(2,1)S(1)} %get-tuple-element.112), channel_id=1, source_target_pairs={{0,8},{1,9},{2,10},{3,11},{4,12},{5,13},{6,14},{7,15},{8,0},{9,1},... | collective-permute-start | bytes 589832 | tf_op jit(solution)/shard_map/ppermute | solution.py:592
  325.0 18.3 %collective-permute-start.32 = (bf16[96,1024]{1,0:T(8,128)(2,1)S(1)}, bf16[96,1024]{1,0:T(8,128)(2,1)S(1)}, u32[]{:S(2)}, u32[]{:S(2)}) collective-permute-start(bf16[96,1024]{1,0:T(8,128)(2,1)S(1)} %get-tuple-element.113), channel_id=1, source_target_pairs={{0,12},{1,13},{2,14},{3,15},{4,8},{5,9},{6,10},{7,11},{8,4},{9,5},... | collective-permute-start | bytes 589832 | tf_op jit(solution)/shard_map/ppermute | solution.py:592
  343.7 4.0 %collective-permute-start.33 = (f32[128,1024]{1,0:T(8,128)S(1)}, f32[128,1024]{1,0:T(8,128)S(1)}, u32[]{:S(2)}, u32[]{:S(2)}) collective-permute-start(f32[128,1024]{1,0:T(8,128)S(1)} %get-tuple-element.108), channel_id=1, source_target_pairs={{0,16},{16,0},{1,17},{17,1},{2,18},{18,2},{3,19},{19,3},{4,20},{20... | collective-permute-start | bytes 1572872 | tf_op jit(solution)/shard_map/ppermute | solution.py:596
  345.5 1.5 collective-permute-start.34
  (60 other events, 475.7 us)
Sparse Core Ops, SparseCore 0:
  34.1 87.8 all-gather.2
  191.7 122.5 reduce-scatter.1
